TPU v7x, 256 devices: a whole 4x4x8 slice. The times are simulated.
256 devices in a mesh: dp: 16 (over z, y_hi), mp: 16 (over x, y_lo, core).
Axes of the slice: x: 4, y: 4 (y_hi: 2, y_lo: 2; y = y_hi * 2 + y_lo), z: 8, core: 2. Of those that a mesh axis runs over, the one named last changes fastest.
Arguments:
- image_features: bfloat16 [1152, 18432], P('mp', 'dp'), may hold values from -6 to 6
- proj_weight: bfloat16 [1152, 1152], P('mp'), may hold values from -0.1875 to 0.1875
- text_embed: bfloat16 [18432, 1152], P(('dp', 'mp')), may hold values from -6 to 6
- text_match: int32 [18432], P(('dp', 'mp')), may hold values from 0 to 18431, as said below
- logit_scale: float32 [1], replicated, may hold values from 4 to 16
- logit_bias: float32 [1], replicated, may hold values from -2.5 to -0.5
Outputs:
- text_grad: bfloat16 [18432, 1152], P(('dp', 'mp'))
- feature_grad: bfloat16 [1152, 18432], P('mp', 'dp')
- proj_grad: float32 [1152, 1152], P('mp')
Inputs may be any that keep to these rules, and one draw needn't show every extreme that they name: text_match[j] is j, or for odd j an even index below j (text j repeats the caption of that image); every even index and the last index map to themselves.
All inputs are finite; a program needn't handle non-finite values.
Results may differ from a plain program's by a relative error of at most 0.02.
Values may be sent and summed in bfloat16 or wider, within the bound.
A program may use at most 64 MiB of HBM per device.

v0:
```python
import jax
import jax.numpy as jnp
from jax import lax
from jax.sharding import PartitionSpec as P

norm_floor = 1e-06


def from_behind(value, axis, by):
    peers = lax.axis_size(axis)
    return lax.ppermute(value, axis, [(i, (i + by) % peers) for i in range(peers)])


def inverse_norm(values):
    return lax.rsqrt(jnp.sum(values * values, axis=1, keepdims=True) + norm_floor)


def norm_backward(values, inverse, upstream):
    along = jnp.sum(values * upstream, axis=1, keepdims=True)
    return inverse * upstream - inverse * inverse * inverse * along * values


def pair_tile(image_unit, image_index, text_unit, text_match, text_index, scaling, offset):
    products = lax.dot_general(
        text_unit, image_unit, (((1,), (1,)), ((), ())), preferred_element_type=jnp.float32
    )
    logits = scaling * products + offset
    positive = (text_index[:, None] == image_index[None, :]) | (
        text_match[:, None] == image_index[None, :]
    )
    signs = jnp.where(positive, 1.0, -1.0).astype(jnp.float32)
    pair_coef = (-signs * scaling * jax.nn.sigmoid(-signs * logits)).astype(jnp.bfloat16)
    text_part = jnp.dot(pair_coef, image_unit, preferred_element_type=jnp.float32)
    image_part = lax.dot_general(
        pair_coef, text_unit, (((0,), (0,)), ((), ())), preferred_element_type=jnp.float32
    )
    return (image_part, text_part)


def pass_partial(partial_sum):
    return from_behind(partial_sum, "dp", 1)


def local(image_features, proj_weight, text_embed, text_match, logit_scale, logit_bias):
    scaling = logit_scale[0]
    offset = logit_bias[0]
    dp_count = lax.axis_size("dp")
    mp_count = lax.axis_size("mp")
    dp_index = lax.axis_index("dp")
    mp_index = lax.axis_index("mp")
    row_count = text_embed.shape[0]
    group_rows = image_features.shape[1]
    embed_width = proj_weight.shape[1]
    image_index = dp_index * group_rows + jnp.arange(group_rows, dtype=jnp.int32)
    feature_piece = lax.all_gather(image_features, "mp", axis=0, tiled=True)
    weight_piece = lax.all_gather(proj_weight, "mp", axis=0, tiled=True)
    projected = lax.dot_general(
        feature_piece, weight_piece, (((0,), (0,)), ((), ())), preferred_element_type=jnp.float32
    )
    image_inverse = inverse_norm(projected)
    image_unit = (projected * image_inverse).astype(jnp.bfloat16)
    text_values = text_embed.astype(jnp.float32)
    text_inverse = inverse_norm(text_values)
    text_unit = (text_values * text_inverse).astype(jnp.bfloat16)
    zeros_image = jnp.zeros((group_rows, embed_width), jnp.float32)
    local_rows = jnp.arange(row_count, dtype=jnp.int32)

    def visit(turn_number, carried):
        text_block, match_block, partial_sum, image_acc = carried
        source = (dp_index - turn_number) % dp_count
        block_index = (source * mp_count + mp_index) * row_count + local_rows
        image_part, text_part = pair_tile(
            image_unit, image_index, text_block, match_block, block_index, scaling, offset
        )
        partial_sum = pass_partial(partial_sum + text_part)
        text_block, match_block = from_behind((text_block, match_block), "dp", 1)
        return (text_block, match_block, partial_sum, image_acc + image_part)

    start_state = (
        text_unit,
        text_match,
        jnp.zeros((row_count, embed_width), jnp.float32),
        zeros_image,
    )
    text_block, match_block, partial_sum, image_acc = lax.fori_loop(
        0, dp_count - 1, visit, start_state
    )
    source = (dp_index + 1) % dp_count
    block_index = (source * mp_count + mp_index) * row_count + local_rows
    image_part, text_part = pair_tile(
        image_unit, image_index, text_block, match_block, block_index, scaling, offset
    )
    image_acc = image_acc + image_part
    text_grad_unit = pass_partial(partial_sum + text_part)
    image_grad_unit = lax.psum(image_acc, "mp")
    grad_projected = norm_backward(projected, image_inverse, image_grad_unit).astype(jnp.bfloat16)
    feature_grad = lax.dot_general(
        proj_weight, grad_projected, (((1,), (1,)), ((), ())), preferred_element_type=jnp.float32
    ).astype(jnp.bfloat16)
    weight_part = jnp.dot(image_features, grad_projected, preferred_element_type=jnp.float32)
    proj_grad = lax.psum(weight_part.astype(jnp.bfloat16), "dp").astype(jnp.float32)
    text_grad = norm_backward(text_values, text_inverse, text_grad_unit).astype(jnp.bfloat16)
    return (text_grad, feature_grad, proj_grad)


def solution(mesh):
    return jax.shard_map(
        local,
        mesh=mesh,
        in_specs=(P("mp", "dp"), P("mp", None), P(("dp", "mp"), None), P(("dp", "mp")), P(), P()),
        out_specs=(P(("dp", "mp"), None), P("mp", "dp"), P("mp", None)),
        check_vma=False,
    )
```

profile of v0, /device:TPU:32, one launch (start us, length us, event | category | flops | bytes accessed | tf_op | source)
XLA Modules:
  0.0 722.9 jit_solution(11790414203602953129)
XLA Ops:
  12.1 37.8 %all-gather.3.cloned.1.call-done = bf16[1152,1152]{1,0:T(8,128)(2,1)} async-done(((bf16[72,1152]{1,0:T(8,128)(2,1)}), bf16[1152,1152]{1,0:T(8,128)(2,1)}) %all-gather.3.cloned.1.call-update) | async-done | bytes 2654224 | tf_op jit(solution)/shard_map/all_gather | solution.py:55
  50.0 39.4 %all-gather.5.cloned.1.call-done = bf16[1152,1152]{1,0:T(8,128)(2,1)} async-done(((bf16[72,1152]{1,0:T(8,128)(2,1)}), bf16[1152,1152]{1,0:T(8,128)(2,1)}) %all-gather.5.cloned.1.call-update) | async-done | bytes 2654224 | tf_op jit(solution)/shard_map/all_gather | solution.py:56
  89.4 6.8 multiply_reduce_fusion.1
  100.5 4.1 copy.9
  104.7 286.7 %while.22 = (s32[]{:T(128)}, bf16[72,1152]{1,0:T(8,128)(2,1)S(1)}, s32[72]{0:T(128)S(1)}, f32[72,1152]{1,0:T(8,128)S(1)}, f32[1152,1152]{1,0:T(8,128)}, /*index=...) while((s32[]{:T(128)}, bf16[72,1152]{1,0:T(8,128)(2,1)S(1)}, ...), condition=%wide.region_3.4_spmd.clone, body=%wide.region_2.3_spmd.clone.sunk | while | flops 577208576 | bytes 19752932 | solution.py:85
  115.7 3.3 convolution_add_fusion.7
  119.0 6.0 collective-permute-done.2
  135.1 5.8 convolution_add_fusion.7
  144.9 4.7 collective-permute-start.1
  154.2 5.8 convolution_add_fusion.7
  164.1 3.9 collective-permute-start.1
  171.8 5.8 convolution_add_fusion.7
  177.6 4.8 collective-permute-done.2
  182.5 3.4 collective-permute-start.1
  189.7 5.8 convolution_add_fusion.7
  195.5 5.3 collective-permute-done.2
  200.9 3.6 collective-permute-start.1
  208.3 5.8 convolution_add_fusion.7
  214.1 5.6 collective-permute-done.2
  226.2 5.8 convolution_add_fusion.7
  236.8 3.9 collective-permute-start.1
  246.8 5.8 convolution_add_fusion.7
  256.6 4.8 collective-permute-start.1
  265.2 5.8 convolution_add_fusion.7
  271.0 6.4 collective-permute-done.2
  283.8 5.8 convolution_add_fusion.7
  289.6 7.1 collective-permute-done.2
  303.0 6.0 collective-permute-start.2
  309.0 5.8 convolution_add_fusion.7
  315.7 3.9 collective-permute-start
  319.7 4.6 collective-permute-start.1
  328.0 5.8 convolution_add_fusion.7
  333.8 3.9 collective-permute-done.2
  344.2 5.8 convolution_add_fusion.7
  350.0 3.9 collective-permute-done.2
  354.0 3.7 collective-permute-start.1
  361.5 5.8 convolution_add_fusion.7
  367.2 3.9 collective-permute-done.2
  371.2 3.5 collective-permute-start.1
  379.0 5.8 convolution_add_fusion.7
  384.8 6.6 collective-permute-done.2
  391.4 7.0 copy.10
  399.0 5.8 convolution_add_fusion.2
  406.2 9.5 %collective-permute-done.3 = f32[72,1152]{1,0:T(8,128)S(1)} collective-permute-done((f32[72,1152]{1,0:T(8,128)S(1)}, f32[72,1152]{1,0:T(8,128)S(1)}, u32[]{:S(2)}, u32[]{:S(2)}) %collective-permute-start.3) | collective-permute-done | bytes 331808 | tf_op jit(solution)/shard_map/ppermute | solution.py:11
  416.7 131.5 %all-reduce.3.cloned.1.call-done = f32[1152,1152]{0,1:T(8,128)} async-done(((f32[1152,1152]{0,1:T(8,128)}), f32[1152,1152]{0,1:T(8,128)}) %all-reduce.3.cloned.1.call-update) | async-done | bytes 5308432 | tf_op jit(solution)/shard_map/psum | solution.py:95
  548.2 4.8 multiply_reduce_fusion
  553.7 3.7 subtract_convert_fusion
  560.5 154.2 %all-reduce.5.cloned.1.call-done = bf16[72,1152]{1,0:T(8,128)(2,1)} async-done(((bf16[72,1152]{1,0:T(8,128)(2,1)}), bf16[72,1152]{1,0:T(8,128)(2,1)}) %all-reduce.5.cloned.1.call-update) | async-done | bytes 165904 | tf_op jit(solution)/shard_map/psum | solution.py:101
  (200 shorter events, 119.0 us)
Async XLA Ops:
  7.2 42.8 %all-gather.3.cloned.1.call-start = ((), (), s32[]{:S(2)}) async-start(), calls=%async_computation | async-start | bytes 2820096 | tf_op jit(solution)/shard_map/all_gather | solution.py:55
  7.9 81.5 %all-gather.5.cloned.1.call-start = ((), (), s32[]{:S(2)}) async-start(), calls=%async_computation.1 | async-start | bytes 2820096 | tf_op jit(solution)/shard_map/all_gather | solution.py:56
  8.6 539.5 %all-reduce.3.cloned.1.call-start = ((), (), s32[]{:S(2)}) async-start(), calls=%async_computation.2 | async-start | bytes 10616832 | tf_op jit(solution)/shard_map/psum | solution.py:95
  104.7 14.3 %collective-permute-start = (bf16[72,1152]{1,0:T(8,128)(2,1)S(1)}, bf16[72,1152]{1,0:T(8,128)(2,1)S(1)}, u32[]{:S(2)}, u32[]{:S(2)}) collective-permute-start(bf16[72,1152]{1,0:T(8,128)(2,1)S(1)} %copy.19), channel_id=1, source_target_pairs={{0,16},{16,32},{32,48},{48,64},{64,80},{80,96},{96,112},{112,128},... | collective-permute-start | bytes 497672 | tf_op jit(solution)/shard_map/while/body/eval_jaxpr/ppermute | solution.py:11
  107.5 11.5 %collective-permute-start.1 = (s32[72]{0:T(128)S(1)}, s32[72]{0:T(128)S(1)}, u32[]{:S(2)}, u32[]{:S(2)}) collective-permute-start(s32[72]{0:T(128)S(1)} %copy.20), channel_id=1, source_target_pairs={{0,16},{16,32},{32,48},{48,64},{64,80},{80,96},{96,112},{112,128},... | collective-permute-start | bytes 872 | tf_op jit(solution)/shard_map/while/body/eval_jaxpr/ppermute | solution.py:11
  113.0 12.0 %collective-permute-start.2 = (f32[72,1152]{1,0:T(8,128)}, f32[72,1152]{1,0:T(8,128)S(1)}, u32[]{:S(2)}, u32[]{:S(2)}) collective-permute-start(f32[72,1152]{1,0:T(8,128)} %convolution_add_fusion.6), channel_id=1, source_target_pairs={{0,16},{16,32},{32,48},{48,64},{64,80},{80,96},{96,112},{112,128},... | collective-permute-start | bytes 995336 | tf_op jit(solution)/shard_map/while/body/eval_jaxpr/ppermute | solution.py:11
  125.0 15.9 %collective-permute-start = (bf16[72,1152]{1,0:T(8,128)(2,1)S(1)}, bf16[72,1152]{1,0:T(8,128)(2,1)S(1)}, u32[]{:S(2)}, u32[]{:S(2)}) collective-permute-start(bf16[72,1152]{1,0:T(8,128)(2,1)S(1)} %copy.19), channel_id=1, source_target_pairs={{0,16},{16,32},{32,48},{48,64},{64,80},{80,96},{96,112},{112,128},... | collective-permute-start | bytes 497672 | tf_op jit(solution)/shard_map/while/body/eval_jaxpr/ppermute | solution.py:11
  126.9 14.0 %collective-permute-start.1 = (s32[72]{0:T(128)S(1)}, s32[72]{0:T(128)S(1)}, u32[]{:S(2)}, u32[]{:S(2)}) collective-permute-start(s32[72]{0:T(128)S(1)} %copy.20), channel_id=1, source_target_pairs={{0,16},{16,32},{32,48},{48,64},{64,80},{80,96},{96,112},{112,128},... | collective-permute-start | bytes 872 | tf_op jit(solution)/shard_map/while/body/eval_jaxpr/ppermute | solution.py:11
  133.3 10.5 %collective-permute-start.2 = (f32[72,1152]{1,0:T(8,128)}, f32[72,1152]{1,0:T(8,128)S(1)}, u32[]{:S(2)}, u32[]{:S(2)}) collective-permute-start(f32[72,1152]{1,0:T(8,128)} %convolution_add_fusion.6), channel_id=1, source_target_pairs={{0,16},{16,32},{32,48},{48,64},{64,80},{80,96},{96,112},{112,128},... | collective-permute-start | bytes 995336 | tf_op jit(solution)/shard_map/while/body/eval_jaxpr/ppermute | solution.py:11
  143.8 16.2 %collective-permute-start = (bf16[72,1152]{1,0:T(8,128)(2,1)S(1)}, bf16[72,1152]{1,0:T(8,128)(2,1)S(1)}, u32[]{:S(2)}, u32[]{:S(2)}) collective-permute-start(bf16[72,1152]{1,0:T(8,128)(2,1)S(1)} %copy.19), channel_id=1, source_target_pairs={{0,16},{16,32},{32,48},{48,64},{64,80},{80,96},{96,112},{112,128},... | collective-permute-start | bytes 497672 | tf_op jit(solution)/shard_map/while/body/eval_jaxpr/ppermute | solution.py:11
  144.9 15.1 %collective-permute-start.1 = (s32[72]{0:T(128)S(1)}, s32[72]{0:T(128)S(1)}, u32[]{:S(2)}, u32[]{:S(2)}) collective-permute-start(s32[72]{0:T(128)S(1)} %copy.20), channel_id=1, source_target_pairs={{0,16},{16,32},{32,48},{48,64},{64,80},{80,96},{96,112},{112,128},... | collective-permute-start | bytes 872 | tf_op jit(solution)/shard_map/while/body/eval_jaxpr/ppermute | solution.py:11
  153.3 9.7 %collective-permute-start.2 = (f32[72,1152]{1,0:T(8,128)}, f32[72,1152]{1,0:T(8,128)S(1)}, u32[]{:S(2)}, u32[]{:S(2)}) collective-permute-start(f32[72,1152]{1,0:T(8,128)} %convolution_add_fusion.6), channel_id=1, source_target_pairs={{0,16},{16,32},{32,48},{48,64},{64,80},{80,96},{96,112},{112,128},... | collective-permute-start | bytes 995336 | tf_op jit(solution)/shard_map/while/body/eval_jaxpr/ppermute | solution.py:11
  163.1 14.5 %collective-permute-start = (bf16[72,1152]{1,0:T(8,128)(2,1)S(1)}, bf16[72,1152]{1,0:T(8,128)(2,1)S(1)}, u32[]{:S(2)}, u32[]{:S(2)}) collective-permute-start(bf16[72,1152]{1,0:T(8,128)(2,1)S(1)} %copy.19), channel_id=1, source_target_pairs={{0,16},{16,32},{32,48},{48,64},{64,80},{80,96},{96,112},{112,128},... | collective-permute-start | bytes 497672 | tf_op jit(solution)/shard_map/while/body/eval_jaxpr/ppermute | solution.py:11
  164.1 13.5 %collective-permute-start.1 = (s32[72]{0:T(128)S(1)}, s32[72]{0:T(128)S(1)}, u32[]{:S(2)}, u32[]{:S(2)}) collective-permute-start(s32[72]{0:T(128)S(1)} %copy.20), channel_id=1, source_target_pairs={{0,16},{16,32},{32,48},{48,64},{64,80},{80,96},{96,112},{112,128},... | collective-permute-start | bytes 872 | tf_op jit(solution)/shard_map/while/body/eval_jaxpr/ppermute | solution.py:11
  171.7 10.7 %collective-permute-start.2 = (f32[72,1152]{1,0:T(8,128)}, f32[72,1152]{1,0:T(8,128)S(1)}, u32[]{:S(2)}, u32[]{:S(2)}) collective-permute-start(f32[72,1152]{1,0:T(8,128)} %convolution_add_fusion.6), channel_id=1, source_target_pairs={{0,16},{16,32},{32,48},{48,64},{64,80},{80,96},{96,112},{112,128},... | collective-permute-start | bytes 995336 | tf_op jit(solution)/shard_map/while/body/eval_jaxpr/ppermute | solution.py:11
  182.4 13.0 %collective-permute-start = (bf16[72,1152]{1,0:T(8,128)(2,1)S(1)}, bf16[72,1152]{1,0:T(8,128)(2,1)S(1)}, u32[]{:S(2)}, u32[]{:S(2)}) collective-permute-start(bf16[72,1152]{1,0:T(8,128)(2,1)S(1)} %copy.19), channel_id=1, source_target_pairs={{0,16},{16,32},{32,48},{48,64},{64,80},{80,96},{96,112},{112,128},... | collective-permute-start | bytes 497672 | tf_op jit(solution)/shard_map/while/body/eval_jaxpr/ppermute | solution.py:11
  182.5 12.9 %collective-permute-start.1 = (s32[72]{0:T(128)S(1)}, s32[72]{0:T(128)S(1)}, u32[]{:S(2)}, u32[]{:S(2)}) collective-permute-start(s32[72]{0:T(128)S(1)} %copy.20), channel_id=1, source_target_pairs={{0,16},{16,32},{32,48},{48,64},{64,80},{80,96},{96,112},{112,128},... | collective-permute-start | bytes 872 | tf_op jit(solution)/shard_map/while/body/eval_jaxpr/ppermute | solution.py:11
  189.6 11.2 %collective-permute-start.2 = (f32[72,1152]{1,0:T(8,128)}, f32[72,1152]{1,0:T(8,128)S(1)}, u32[]{:S(2)}, u32[]{:S(2)}) collective-permute-start(f32[72,1152]{1,0:T(8,128)} %convolution_add_fusion.6), channel_id=1, source_target_pairs={{0,16},{16,32},{32,48},{48,64},{64,80},{80,96},{96,112},{112,128},... | collective-permute-start | bytes 995336 | tf_op jit(solution)/shard_map/while/body/eval_jaxpr/ppermute | solution.py:11
  200.8 13.3 %collective-permute-start = (bf16[72,1152]{1,0:T(8,128)(2,1)S(1)}, bf16[72,1152]{1,0:T(8,128)(2,1)S(1)}, u32[]{:S(2)}, u32[]{:S(2)}) collective-permute-start(bf16[72,1152]{1,0:T(8,128)(2,1)S(1)} %copy.19), channel_id=1, source_target_pairs={{0,16},{16,32},{32,48},{48,64},{64,80},{80,96},{96,112},{112,128},... | collective-permute-start | bytes 497672 | tf_op jit(solution)/shard_map/while/body/eval_jaxpr/ppermute | solution.py:11
  200.9 13.2 %collective-permute-start.1 = (s32[72]{0:T(128)S(1)}, s32[72]{0:T(128)S(1)}, u32[]{:S(2)}, u32[]{:S(2)}) collective-permute-start(s32[72]{0:T(128)S(1)} %copy.20), channel_id=1, source_target_pairs={{0,16},{16,32},{32,48},{48,64},{64,80},{80,96},{96,112},{112,128},... | collective-permute-start | bytes 872 | tf_op jit(solution)/shard_map/while/body/eval_jaxpr/ppermute | solution.py:11
  208.2 11.5 %collective-permute-start.2 = (f32[72,1152]{1,0:T(8,128)}, f32[72,1152]{1,0:T(8,128)S(1)}, u32[]{:S(2)}, u32[]{:S(2)}) collective-permute-start(f32[72,1152]{1,0:T(8,128)} %convolution_add_fusion.6), channel_id=1, source_target_pairs={{0,16},{16,32},{32,48},{48,64},{64,80},{80,96},{96,112},{112,128},... | collective-permute-start | bytes 995336 | tf_op jit(solution)/shard_map/while/body/eval_jaxpr/ppermute | solution.py:11
  219.8 12.2 %collective-permute-start = (bf16[72,1152]{1,0:T(8,128)(2,1)S(1)}, bf16[72,1152]{1,0:T(8,128)(2,1)S(1)}, u32[]{:S(2)}, u32[]{:S(2)}) collective-permute-start(bf16[72,1152]{1,0:T(8,128)(2,1)S(1)} %copy.19), channel_id=1, source_target_pairs={{0,16},{16,32},{32,48},{48,64},{64,80},{80,96},{96,112},{112,128},... | collective-permute-start | bytes 497672 | tf_op jit(solution)/shard_map/while/body/eval_jaxpr/ppermute | solution.py:11
  219.9 12.1 %collective-permute-start.1 = (s32[72]{0:T(128)S(1)}, s32[72]{0:T(128)S(1)}, u32[]{:S(2)}, u32[]{:S(2)}) collective-permute-start(s32[72]{0:T(128)S(1)} %copy.20), channel_id=1, source_target_pairs={{0,16},{16,32},{32,48},{48,64},{64,80},{80,96},{96,112},{112,128},... | collective-permute-start | bytes 872 | tf_op jit(solution)/shard_map/while/body/eval_jaxpr/ppermute | solution.py:11
  223.7 11.2 %collective-permute-start.2 = (f32[72,1152]{1,0:T(8,128)}, f32[72,1152]{1,0:T(8,128)S(1)}, u32[]{:S(2)}, u32[]{:S(2)}) collective-permute-start(f32[72,1152]{1,0:T(8,128)} %convolution_add_fusion.6), channel_id=1, source_target_pairs={{0,16},{16,32},{32,48},{48,64},{64,80},{80,96},{96,112},{112,128},... | collective-permute-start | bytes 995336 | tf_op jit(solution)/shard_map/while/body/eval_jaxpr/ppermute | solution.py:11
  234.9 17.6 %collective-permute-start = (bf16[72,1152]{1,0:T(8,128)(2,1)S(1)}, bf16[72,1152]{1,0:T(8,128)(2,1)S(1)}, u32[]{:S(2)}, u32[]{:S(2)}) collective-permute-start(bf16[72,1152]{1,0:T(8,128)(2,1)S(1)} %copy.19), channel_id=1, source_target_pairs={{0,16},{16,32},{32,48},{48,64},{64,80},{80,96},{96,112},{112,128},... | collective-permute-start | bytes 497672 | tf_op jit(solution)/shard_map/while/body/eval_jaxpr/ppermute | solution.py:11
  236.8 15.7 %collective-permute-start.1 = (s32[72]{0:T(128)S(1)}, s32[72]{0:T(128)S(1)}, u32[]{:S(2)}, u32[]{:S(2)}) collective-permute-start(s32[72]{0:T(128)S(1)} %copy.20), channel_id=1, source_target_pairs={{0,16},{16,32},{32,48},{48,64},{64,80},{80,96},{96,112},{112,128},... | collective-permute-start | bytes 872 | tf_op jit(solution)/shard_map/while/body/eval_jaxpr/ppermute | solution.py:11
  244.4 9.7 %collective-permute-start.2 = (f32[72,1152]{1,0:T(8,128)}, f32[72,1152]{1,0:T(8,128)S(1)}, u32[]{:S(2)}, u32[]{:S(2)}) collective-permute-start(f32[72,1152]{1,0:T(8,128)} %convolution_add_fusion.6), channel_id=1, source_target_pairs={{0,16},{16,32},{32,48},{48,64},{64,80},{80,96},{96,112},{112,128},... | collective-permute-start | bytes 995336 | tf_op jit(solution)/shard_map/while/body/eval_jaxpr/ppermute | solution.py:11
  254.2 16.8 %collective-permute-start = (bf16[72,1152]{1,0:T(8,128)(2,1)S(1)}, bf16[72,1152]{1,0:T(8,128)(2,1)S(1)}, u32[]{:S(2)}, u32[]{:S(2)}) collective-permute-start(bf16[72,1152]{1,0:T(8,128)(2,1)S(1)} %copy.19), channel_id=1, source_target_pairs={{0,16},{16,32},{32,48},{48,64},{64,80},{80,96},{96,112},{112,128},... | collective-permute-start | bytes 497672 | tf_op jit(solution)/shard_map/while/body/eval_jaxpr/ppermute | solution.py:11
  256.6 14.3 %collective-permute-start.1 = (s32[72]{0:T(128)S(1)}, s32[72]{0:T(128)S(1)}, u32[]{:S(2)}, u32[]{:S(2)}) collective-permute-start(s32[72]{0:T(128)S(1)} %copy.20), channel_id=1, source_target_pairs={{0,16},{16,32},{32,48},{48,64},{64,80},{80,96},{96,112},{112,128},... | collective-permute-start | bytes 872 | tf_op jit(solution)/shard_map/while/body/eval_jaxpr/ppermute | solution.py:11
  265.1 12.3 %collective-permute-start.2 = (f32[72,1152]{1,0:T(8,128)}, f32[72,1152]{1,0:T(8,128)S(1)}, u32[]{:S(2)}, u32[]{:S(2)}) collective-permute-start(f32[72,1152]{1,0:T(8,128)} %convolution_add_fusion.6), channel_id=1, source_target_pairs={{0,16},{16,32},{32,48},{48,64},{64,80},{80,96},{96,112},{112,128},... | collective-permute-start | bytes 995336 | tf_op jit(solution)/shard_map/while/body/eval_jaxpr/ppermute | solution.py:11
  277.4 12.1 %collective-permute-start = (bf16[72,1152]{1,0:T(8,128)(2,1)S(1)}, bf16[72,1152]{1,0:T(8,128)(2,1)S(1)}, u32[]{:S(2)}, u32[]{:S(2)}) collective-permute-start(bf16[72,1152]{1,0:T(8,128)(2,1)S(1)} %copy.19), channel_id=1, source_target_pairs={{0,16},{16,32},{32,48},{48,64},{64,80},{80,96},{96,112},{112,128},... | collective-permute-start | bytes 497672 | tf_op jit(solution)/shard_map/while/body/eval_jaxpr/ppermute | solution.py:11
  277.5 12.0 %collective-permute-start.1 = (s32[72]{0:T(128)S(1)}, s32[72]{0:T(128)S(1)}, u32[]{:S(2)}, u32[]{:S(2)}) collective-permute-start(s32[72]{0:T(128)S(1)} %copy.20), channel_id=1, source_target_pairs={{0,16},{16,32},{32,48},{48,64},{64,80},{80,96},{96,112},{112,128},... | collective-permute-start | bytes 872 | tf_op jit(solution)/shard_map/while/body/eval_jaxpr/ppermute | solution.py:11
  283.7 13.0 %collective-permute-start.2 = (f32[72,1152]{1,0:T(8,128)}, f32[72,1152]{1,0:T(8,128)S(1)}, u32[]{:S(2)}, u32[]{:S(2)}) collective-permute-start(f32[72,1152]{1,0:T(8,128)} %convolution_add_fusion.6), channel_id=1, source_target_pairs={{0,16},{16,32},{32,48},{48,64},{64,80},{80,96},{96,112},{112,128},... | collective-permute-start | bytes 995336 | tf_op jit(solution)/shard_map/while/body/eval_jaxpr/ppermute | solution.py:11
  296.6 18.1 %collective-permute-start = (bf16[72,1152]{1,0:T(8,128)(2,1)S(1)}, bf16[72,1152]{1,0:T(8,128)(2,1)S(1)}, u32[]{:S(2)}, u32[]{:S(2)}) collective-permute-start(bf16[72,1152]{1,0:T(8,128)(2,1)S(1)} %copy.19), channel_id=1, source_target_pairs={{0,16},{16,32},{32,48},{48,64},{64,80},{80,96},{96,112},{112,128},... | collective-permute-start | bytes 497672 | tf_op jit(solution)/shard_map/while/body/eval_jaxpr/ppermute | solution.py:11
  296.8 18.0 %collective-permute-start.1 = (s32[72]{0:T(128)S(1)}, s32[72]{0:T(128)S(1)}, u32[]{:S(2)}, u32[]{:S(2)}) collective-permute-start(s32[72]{0:T(128)S(1)} %copy.20), channel_id=1, source_target_pairs={{0,16},{16,32},{32,48},{48,64},{64,80},{80,96},{96,112},{112,128},... | collective-permute-start | bytes 872 | tf_op jit(solution)/shard_map/while/body/eval_jaxpr/ppermute | solution.py:11
  303.0 12.7 %collective-permute-start.2 = (f32[72,1152]{1,0:T(8,128)}, f32[72,1152]{1,0:T(8,128)S(1)}, u32[]{:S(2)}, u32[]{:S(2)}) collective-permute-start(f32[72,1152]{1,0:T(8,128)} %convolution_add_fusion.6), channel_id=1, source_target_pairs={{0,16},{16,32},{32,48},{48,64},{64,80},{80,96},{96,112},{112,128},... | collective-permute-start | bytes 995336 | tf_op jit(solution)/shard_map/while/body/eval_jaxpr/ppermute | solution.py:11
  315.7 18.1 %collective-permute-start = (bf16[72,1152]{1,0:T(8,128)(2,1)S(1)}, bf16[72,1152]{1,0:T(8,128)(2,1)S(1)}, u32[]{:S(2)}, u32[]{:S(2)}) collective-permute-start(bf16[72,1152]{1,0:T(8,128)(2,1)S(1)} %copy.19), channel_id=1, source_target_pairs={{0,16},{16,32},{32,48},{48,64},{64,80},{80,96},{96,112},{112,128},... | collective-permute-start | bytes 497672 | tf_op jit(solution)/shard_map/while/body/eval_jaxpr/ppermute | solution.py:11
  319.7 14.1 %collective-permute-start.1 = (s32[72]{0:T(128)S(1)}, s32[72]{0:T(128)S(1)}, u32[]{:S(2)}, u32[]{:S(2)}) collective-permute-start(s32[72]{0:T(128)S(1)} %copy.20), channel_id=1, source_target_pairs={{0,16},{16,32},{32,48},{48,64},{64,80},{80,96},{96,112},{112,128},... | collective-permute-start | bytes 872 | tf_op jit(solution)/shard_map/while/body/eval_jaxpr/ppermute | solution.py:11
  327.9 9.7 %collective-permute-start.2 = (f32[72,1152]{1,0:T(8,128)}, f32[72,1152]{1,0:T(8,128)S(1)}, u32[]{:S(2)}, u32[]{:S(2)}) collective-permute-start(f32[72,1152]{1,0:T(8,128)} %convolution_add_fusion.6), channel_id=1, source_target_pairs={{0,16},{16,32},{32,48},{48,64},{64,80},{80,96},{96,112},{112,128},... | collective-permute-start | bytes 995336 | tf_op jit(solution)/shard_map/while/body/eval_jaxpr/ppermute | solution.py:11
  337.7 12.4 %collective-permute-start = (bf16[72,1152]{1,0:T(8,128)(2,1)S(1)}, bf16[72,1152]{1,0:T(8,128)(2,1)S(1)}, u32[]{:S(2)}, u32[]{:S(2)}) collective-permute-start(bf16[72,1152]{1,0:T(8,128)(2,1)S(1)} %copy.19), channel_id=1, source_target_pairs={{0,16},{16,32},{32,48},{48,64},{64,80},{80,96},{96,112},{112,128},... | collective-permute-start | bytes 497672 | tf_op jit(solution)/shard_map/while/body/eval_jaxpr/ppermute | solution.py:11
  337.8 12.3 %collective-permute-start.1 = (s32[72]{0:T(128)S(1)}, s32[72]{0:T(128)S(1)}, u32[]{:S(2)}, u32[]{:S(2)}) collective-permute-start(s32[72]{0:T(128)S(1)} %copy.20), channel_id=1, source_target_pairs={{0,16},{16,32},{32,48},{48,64},{64,80},{80,96},{96,112},{112,128},... | collective-permute-start | bytes 872 | tf_op jit(solution)/shard_map/while/body/eval_jaxpr/ppermute | solution.py:11
  353.9 13.3 %collective-permute-start = (bf16[72,1152]{1,0:T(8,128)(2,1)S(1)}, bf16[72,1152]{1,0:T(8,128)(2,1)S(1)}, u32[]{:S(2)}, u32[]{:S(2)}) collective-permute-start(bf16[72,1152]{1,0:T(8,128)(2,1)S(1)} %copy.19), channel_id=1, source_target_pairs={{0,16},{16,32},{32,48},{48,64},{64,80},{80,96},{96,112},{112,128},... | collective-permute-start | bytes 497672 | tf_op jit(solution)/shard_map/while/body/eval_jaxpr/ppermute | solution.py:11
  354.0 13.2 %collective-permute-start.1 = (s32[72]{0:T(128)S(1)}, s32[72]{0:T(128)S(1)}, u32[]{:S(2)}, u32[]{:S(2)}) collective-permute-start(s32[72]{0:T(128)S(1)} %copy.20), channel_id=1, source_target_pairs={{0,16},{16,32},{32,48},{48,64},{64,80},{80,96},{96,112},{112,128},... | collective-permute-start | bytes 872 | tf_op jit(solution)/shard_map/while/body/eval_jaxpr/ppermute | solution.py:11
  371.1 13.7 %collective-permute-start = (bf16[72,1152]{1,0:T(8,128)(2,1)S(1)}, bf16[72,1152]{1,0:T(8,128)(2,1)S(1)}, u32[]{:S(2)}, u32[]{:S(2)}) collective-permute-start(bf16[72,1152]{1,0:T(8,128)(2,1)S(1)} %copy.19), channel_id=1, source_target_pairs={{0,16},{16,32},{32,48},{48,64},{64,80},{80,96},{96,112},{112,128},... | collective-permute-start | bytes 497672 | tf_op jit(solution)/shard_map/while/body/eval_jaxpr/ppermute | solution.py:11
  371.2 13.6 %collective-permute-start.1 = (s32[72]{0:T(128)S(1)}, s32[72]{0:T(128)S(1)}, u32[]{:S(2)}, u32[]{:S(2)}) collective-permute-start(s32[72]{0:T(128)S(1)} %copy.20), channel_id=1, source_target_pairs={{0,16},{16,32},{32,48},{48,64},{64,80},{80,96},{96,112},{112,128},... | collective-permute-start | bytes 872 | tf_op jit(solution)/shard_map/while/body/eval_jaxpr/ppermute | solution.py:11
  378.4 13.0 %collective-permute-start.2 = (f32[72,1152]{1,0:T(8,128)}, f32[72,1152]{1,0:T(8,128)S(1)}, u32[]{:S(2)}, u32[]{:S(2)}) collective-permute-start(f32[72,1152]{1,0:T(8,128)} %convolution_add_fusion.6), channel_id=1, source_target_pairs={{0,16},{16,32},{32,48},{48,64},{64,80},{80,96},{96,112},{112,128},... | collective-permute-start | bytes 995336 | tf_op jit(solution)/shard_map/while/body/eval_jaxpr/ppermute | solution.py:11
  404.9 309.8 %all-reduce.5.cloned.1.call-start = ((), (), s32[]{:S(2)}) async-start(), calls=%async_computation.3 | async-start | bytes 331776 | tf_op jit(solution)/shard_map/psum | solution.py:101
  405.9 9.8 %collective-permute-start.3 = (f32[72,1152]{1,0:T(8,128)S(1)}, f32[72,1152]{1,0:T(8,128)S(1)}, u32[]{:S(2)}, u32[]{:S(2)}) collective-permute-start(f32[72,1152]{1,0:T(8,128)S(1)} %convolution_add_fusion.3), channel_id=1, source_target_pairs={{0,16},{16,32},{32,48},{48,64},{64,80},{80,96},{96,112},{112,128},... | collective-permute-start | bytes 995336 | tf_op jit(solution)/shard_map/ppermute | solution.py:11
  (9 other events, 56.9 us)
Sparse Core Ops, SparseCore 0:
  9.9 40.0 all-gather.2
  51.8 37.5 all-gather.4
  405.0 143.1 all-reduce.2
  559.4 155.2 all-reduce.4
where the time goes:
time: 725 us; the launch traced here: 723 us
  waiting for transfers between devices  439 us (61%)
  matrix products  156 us (22%)
  starting transfers between devices  82.1 us (11%)
  other arithmetic  15.3 us (2%)
  between operations  15.2 us (2%)
  local copies, waits for them, and re-layouts  14.5 us (2%)
    psum x1, waiting for transfers between devices, local(): lax.psum(weight_part.astype(jnp.bfloat16), 'dp').astype(jnp.float32)  154 us
    psum x1, waiting for transfers between devices, local(): image_grad_unit = lax.psum(image_acc, 'mp')  131 us
    dot_general x16, matrix products, pair_tile(): lax.dot_general(pair_coef, text_unit, (((0,), (0,)), ((), ())), preferred...  89.8 us
    ppermute x46, starting transfers between devices, from_behind(): lax.ppermute(value, axis, [(i, (i + by) % peers) for i in range(peers)])  82 us
    ppermute x46, waiting for transfers between devices, from_behind(): lax.ppermute(value, axis, [(i, (i + by) % peers) for i in range(peers)])  74.6 us
    all_gather x1, waiting for transfers between devices, local(): weight_piece = lax.all_gather(proj_weight, 'mp', axis=0, tiled=True)  39.4 us
    all_gather x1, waiting for transfers between devices, local(): feature_piece = lax.all_gather(image_features, 'mp', axis=0, tiled=True)  37.8 us
    dot_general x16, matrix products, pair_tile(): lax.dot_general(text_unit, image_unit, (((1,), (1,)), ((), ())), preferre...  35.6 us
  transfers between devices with their start and end apart: 50, of which 20 were waited for; matrix products, arithmetic and copies ran while one was open for 20% of the time, Pallas kernels for 0%

commit v1 on v0

v1 whole, which is shorter than its diff:
```python
import functools

import jax
import jax.numpy as jnp
from jax import lax
from jax.experimental import pallas as pl
from jax.experimental.pallas import tpu as pltpu
from jax.sharding import PartitionSpec as P

MESH = pl.DeviceIdType.MESH
norm_floor = 1e-06
f32, bf16 = jnp.float32, jnp.bfloat16

ZS, XS = 8, 4
ROWS = 72
PAD = 80
BLOCK = 144
HEAD = 80
GROUP = 1152
EMBED = 1152
CHUNK = 288
TILE = 384
TEXT_ORDER = (4, -3, 3, -2, 2, -1, 1, 0)
TEXT_POS = {step: at for at, step in enumerate(TEXT_ORDER)}
IMAGE_ORDER = (2, 1, 3, 0)
PIECES, PIECE_ROWS, PIECE_COLS = 15, 16, 384
SEMS = 160


def inverse_norm(values):
    return lax.rsqrt(jnp.sum(values * values, axis=1, keepdims=True) + norm_floor)


def norm_backward(values, inverse, upstream):
    along = jnp.sum(values * upstream, axis=1, keepdims=True)
    return inverse * upstream - inverse * inverse * inverse * along * values


def kernel(
    scale_ref, bias_ref, f_ref, w_ref, t_ref, m_ref,
    tg_ref, fg_ref, pg_ref,
    xsend, xrecv, fw, tsend, trecv, msend, mrecv, tn, mt, mcol, proj, unit, logits, coef, dt, du,
    tout, tra, tlb, tr, tl, ysend_t, yrecv_t,
    csend, crecv, xout, xra, xlb, xr, xl, yout, yin, gp,
    ws, wr, wa,
    send_sem, recv_sem,
):
    d, m = lax.axis_index("dp"), lax.axis_index("mp")
    z, yhi = d // 2, d % 2
    x, ylo, core = m // 4, (m // 2) % 2, m % 2

    def at_z(step):
        return {"dp": lax.rem(z + step + ZS, ZS) * 2 + yhi, "mp": m}

    def at_x(step):
        return {"dp": d, "mp": lax.rem(x + step + XS, XS) * 4 + ylo * 2 + core}

    other_yhi = {"dp": z * 2 + (1 - yhi), "mp": m}
    other_ylo = {"dp": d, "mp": x * 4 + (1 - ylo) * 2 + core}
    sibling = {"dp": d, "mp": x * 4 + ylo * 2 + (1 - core)}

    def dp_at(index):
        return {"dp": index, "mp": m}

    barrier = pltpu.get_barrier_semaphore()
    partners = [sibling, other_ylo, at_x(1), at_x(-1)]
    partners += [dp_at(lax.rem(d + step, 16)) for step in range(1, 16)]
    for partner in partners:
        pl.semaphore_signal(barrier, inc=1, device_id=partner, device_id_type=MESH)

    keys = {}

    def key(name):
        return keys.setdefault(name, len(keys))

    def describe(name, src, dst, target):
        k = key(name)
        return pltpu.make_async_remote_copy(
            src_ref=src, dst_ref=dst, send_sem=send_sem.at[k], recv_sem=recv_sem.at[k],
            device_id=target, device_id_type=MESH,
        )

    sent = []

    def start(name, src, dst, target):
        copy = describe(name, src, dst, target)
        copy.start()
        sent.append(copy)

    def arrived(name, dst, target=sibling):
        describe(name, dst, dst, target).wait_recv()

    f_mine, w_mine = f_ref[...].astype(f32), w_ref[...].astype(f32)
    is_first = core == 0
    pad_rows = jnp.zeros((PAD - ROWS, EMBED), f32)
    xsend[...] = jnp.concatenate([jnp.where(is_first, w_mine, f_mine), pad_rows]).astype(bf16)
    text_values = t_ref[...].astype(f32)
    text_inverse = inverse_norm(text_values)
    text_mine = text_values * text_inverse
    tsend[...] = jnp.concatenate([text_mine, pad_rows]).astype(bf16)
    msend[...] = jnp.zeros_like(msend)
    msend[0:1, 0:ROWS] = m_ref[...]
    pl.semaphore_wait(barrier, len(partners))

    start("x0", xsend, xrecv, sibling)
    start("t0", tsend, trecv, other_yhi)
    start("m0", msend, mrecv, other_yhi)

    def slot(index, count=1):
        return pl.ds(index * BLOCK, count * BLOCK)

    def mine(index):
        return fw.at[core, slot(index)]

    def share(index):
        start(("fs", index), mine(index), mine(index), sibling)

    arrived("x0", xrecv)
    own = jnp.where(is_first, f_mine, w_mine)
    theirs = xrecv[...].astype(f32)[:ROWS]
    fw[core, slot(0), :] = jnp.concatenate(
        [jnp.where(is_first, own, theirs), jnp.where(is_first, theirs, own)]
    ).astype(bf16)
    start(("fx", 4), mine(0), mine(4), at_x(1))
    start(("fx", 2), mine(0), mine(2), at_x(-1))
    start(("fx", 1), mine(0), mine(1), other_ylo)
    share(0)

    def text_at(step):
        return pl.ds(TEXT_POS[step] * BLOCK, BLOCK)

    def text_forward(step, target, new_step):
        start(("t", new_step), tn.at[text_at(step)], tn.at[text_at(new_step)], target)
        start(("m", new_step), mt.at[TEXT_POS[step]], mt.at[TEXT_POS[new_step]], target)

    def text_arrived(step):
        arrived(("t", step), tn.at[text_at(step)])
        arrived(("m", step), mt.at[TEXT_POS[step]])

    is_low = yhi == 0
    arrived("t0", trecv)
    arrived("m0", mrecv)
    theirs = trecv[...].astype(f32)[:ROWS]
    text_mine = tsend[...].astype(f32)[:ROWS]
    tn[text_at(0), :] = jnp.concatenate(
        [jnp.where(is_low, text_mine, theirs), jnp.where(is_low, theirs, text_mine)]
    ).astype(bf16)
    match_mine, match_theirs = msend[0:1, :], mrecv[0:1, :]
    mt[TEXT_POS[0], 0:1, :] = jnp.where(is_low, match_mine, match_theirs)
    mt[TEXT_POS[0], 1:2, :] = jnp.where(is_low, match_theirs, match_mine)
    mt[TEXT_POS[0], 2:8, :] = jnp.zeros((6, 128), jnp.int32)
    text_forward(0, at_z(1), -1)
    text_forward(0, at_z(-1), 1)

    arrived(("fx", 1), mine(1))
    start(("fx", 5), mine(1), mine(5), at_x(1))
    start(("fx", 3), mine(1), mine(3), at_x(-1))
    share(1)
    arrived(("fx", 4), mine(4))
    start(("fx", 6), mine(4), mine(6), at_x(1))
    share(4)
    arrived(("fx", 2), mine(2))
    share(2)
    text_arrived(-1)
    text_forward(-1, at_z(1), -2)
    text_arrived(1)
    text_forward(1, at_z(-1), 2)
    arrived(("fx", 3), mine(3))
    start(("fx", 7), mine(3), mine(7), at_x(-1))
    share(3)
    arrived(("fx", 5), mine(5))
    share(5)
    text_arrived(-2)
    text_forward(-2, at_z(1), -3)
    text_arrived(2)
    text_forward(2, at_z(-1), 3)
    arrived(("fx", 6), mine(6))
    share(6)
    arrived(("fx", 7), mine(7))
    share(7)

    def far_text(step, start_row, rows, target):
        src = tn.at[pl.ds(TEXT_POS[step] * BLOCK + start_row, rows)]
        dst = tn.at[pl.ds(TEXT_POS[4] * BLOCK + start_row, rows)]
        return src, dst

    text_arrived(-3)
    src, dst_head = far_text(-3, 0, HEAD, None)
    start(("t", 4, 0), src, dst_head, at_z(1))
    start(("m", 4), mt.at[TEXT_POS[-3]], mt.at[TEXT_POS[4]], at_z(1))
    text_arrived(3)
    src, dst_tail = far_text(3, HEAD, BLOCK - HEAD, None)
    start(("t", 4, 1), src, dst_tail, at_z(-1))

    for index in range(8):
        arrived(("fs", index), fw.at[1 - core, slot(index)])

    def project(tile, _):
        columns = pl.ds(pl.multiple_of(tile * TILE, TILE), TILE)
        values = lax.dot_general(
            fw[0, :, columns], fw[1], (((0,), (0,)), ((), ())), preferred_element_type=f32
        )
        normal = (values * inverse_norm(values)).astype(bf16)
        for part in range(TILE // 96):
            piece = tile * (TILE // 96) + part
            away = lax.rem(piece // 3 - x + XS, XS)
            place = jnp.where(away == 2, 0, jnp.where(away == 1, 1, jnp.where(away == 3, 2, 3)))
            row = pl.multiple_of(place * CHUNK + (piece % 3) * 96, 96)
            proj[pl.ds(row, 96), :] = values[part * 96:(part + 1) * 96]
            unit[pl.ds(row, 96), :] = normal[part * 96:(part + 1) * 96]
        return 0

    lax.fori_loop(0, GROUP // TILE, project, 0)

    lane = lax.broadcasted_iota(jnp.int32, (1, GROUP), 1)
    image_index = jnp.zeros_like(lane)
    for place, away in enumerate(IMAGE_ORDER):
        base = d * GROUP + lax.rem(x + away, XS) * CHUNK - place * CHUNK
        image_index = jnp.where(lane // CHUNK == place, base + lane, image_index)

    arrived(("t", 4, 0), dst_head)
    arrived(("t", 4, 1), dst_tail)
    arrived(("m", 4), mt.at[TEXT_POS[4]])

    row_number = lax.broadcasted_iota(jnp.int32, (ROWS, 128), 0)
    for place, step in enumerate(TEXT_ORDER):
        from_z = lax.rem(z + step + ZS, ZS)
        for high in range(2):
            row = mt[place, high:high + 1, :]
            column = jnp.transpose(jnp.broadcast_to(row, (128, 128)))[:ROWS]
            rows = pl.ds(place * BLOCK + high * ROWS, ROWS)
            mcol[0, rows, :] = column
            mcol[1, rows, :] = ((from_z * 2 + high) * 16 + m) * ROWS + row_number

    scaling, offset = scale_ref[0], bias_ref[0]

    def pairs(chunk):
        rows = pl.ds(chunk * CHUNK, CHUNK)
        logits[...] = lax.dot_general(
            tn[rows, :], unit[...], (((1,), (1,)), ((), ())), preferred_element_type=f32
        )

        def coefficients(step, _):
            at = pl.multiple_of(step * 16, 16)
            here = pl.ds(chunk * CHUNK + at, 16)
            match = mcol[0, here, 0:1]
            index = mcol[1, here, 0:1]
            positive = (index == image_index) | (match == image_index)
            factor = jnp.where(positive, -scaling, scaling)
            shift = jnp.where(positive, -offset, offset)
            values = factor * logits[pl.ds(at, 16), :] + shift
            coef[here, :] = (factor / (1.0 + jnp.exp(-values))).astype(bf16)
            return 0

        lax.fori_loop(0, CHUNK // 16, coefficients, 0)
        dt[rows, :] = jnp.dot(coef[rows, :], unit[...], preferred_element_type=f32)

    def text_partial(step):
        return dt[text_at(step), :]

    def text_out(step, values, name, dst, target):
        place = TEXT_POS[step]
        tout[place] = values.astype(bf16)
        start(name, tout.at[place], dst, target)

    pairs(0)
    tout[0] = text_partial(4).astype(bf16)
    start("tra", tout.at[0, pl.ds(0, HEAD)], tra, at_z(1))
    start("tlb", tout.at[0, pl.ds(HEAD, BLOCK - HEAD)], tlb, at_z(-1))
    pairs(1)
    arrived("tlb", tlb)
    values = text_partial(-3)
    values = jnp.concatenate([values[:HEAD], values[HEAD:] + tlb[...].astype(f32)])
    text_out(-3, values, ("tl", 0), tl.at[0], at_z(-1))
    arrived("tra", tra)
    values = text_partial(3)
    values = jnp.concatenate([values[:HEAD] + tra[...].astype(f32), values[HEAD:]])
    text_out(3, values, ("tr", 0), tr.at[0], at_z(1))
    pairs(2)
    pairs(3)

    def image_tile(tile):
        columns = pl.ds(tile * TILE, TILE)
        du[columns, :] = lax.dot_general(
            coef[:, columns], tn[...], (((0,), (0,)), ((), ())), preferred_element_type=f32
        )

    def image_block(place, which):
        return pl.ds(pl.multiple_of(place * CHUNK + which * BLOCK, BLOCK), BLOCK)

    def to_sibling(place):
        csend[place] = du[image_block(place, 1 - core), :].astype(bf16)
        start(("c", place), csend.at[place], crecv.at[place], sibling)

    def with_sibling(place):
        arrived(("c", place), crecv.at[place])
        return du[image_block(place, core), :] + crecv[place].astype(f32)

    def text_step(index):
        arrived(("tr", 1 - index), tr.at[1 - index])
        step = index + 1
        text_out(
            step, text_partial(step) + tr[1 - index].astype(f32), ("tr", 2 - index), tr.at[2 - index], at_z(1)
        )
        arrived(("tl", 1 - index), tl.at[1 - index])
        text_out(
            -step, text_partial(-step) + tl[1 - index].astype(f32), ("tl", 2 - index), tl.at[2 - index], at_z(-1)
        )

    image_tile(0)
    to_sibling(0)
    image_tile(1)
    to_sibling(1)
    xout[0] = with_sibling(0).astype(bf16)
    start("xra", xout.at[0, pl.ds(0, HEAD)], xra, at_x(1))
    start("xlb", xout.at[0, pl.ds(HEAD, BLOCK - HEAD)], xlb, at_x(-1))
    image_tile(2)
    to_sibling(2)
    to_sibling(3)
    text_step(1)
    values = with_sibling(1)
    arrived("xra", xra)
    xout[1] = jnp.concatenate([values[:HEAD] + xra[...].astype(f32), values[HEAD:]]).astype(bf16)
    start("xr", xout.at[1], xr, at_x(1))
    values = with_sibling(2)
    arrived("xlb", xlb)
    xout[2] = jnp.concatenate([values[:HEAD], values[HEAD:] + xlb[...].astype(f32)]).astype(bf16)
    start("xl", xout.at[2], xl, at_x(-1))
    values = with_sibling(3)
    arrived("xr", xr)
    arrived("xl", xl)
    values = values + xr[...].astype(f32) + xl[...].astype(f32)
    yout[...] = values.astype(bf16)

    def gp_block(from_x, which, start_row=0, rows=BLOCK):
        first = pl.multiple_of(from_x * CHUNK + which * BLOCK + start_row, 16)
        return gp.at[pl.ds(first, rows)]

    owner = ylo == core
    mine_gp = gp_block(x, core)
    to_owner = describe("yo", yout, yin, other_ylo)
    from_owner = describe("yg", mine_gp, mine_gp, other_ylo)

    @pl.when(jnp.logical_not(owner))
    def _():
        to_owner.start()

    text_step(0)

    @pl.when(owner)
    def _():
        to_owner.wait_recv()
        total = values + yin[...].astype(f32)
        projected = proj[image_block(3, core), :]
        first = pl.multiple_of(x * CHUNK + core * BLOCK, 16)
        gp[pl.ds(first, BLOCK), :] = norm_backward(
            projected, inverse_norm(projected), total
        ).astype(bf16)
        from_owner.start()

    @pl.when(jnp.logical_not(owner))
    def _():
        from_owner.wait_recv()

    left_x, right_x, far_x = lax.rem(x + 3, XS), lax.rem(x + 1, XS), lax.rem(x + 2, XS)
    tail_rows = BLOCK - HEAD
    start("gr", mine_gp, mine_gp, at_x(1))
    start("gl", mine_gp, mine_gp, at_x(-1))
    start("gs0", mine_gp, mine_gp, sibling)

    arrived(("tr", 2), tr.at[2])
    arrived(("tl", 2), tl.at[2])
    total = text_partial(0) + tr[2].astype(f32) + tl[2].astype(f32)
    for_other = jnp.where(is_low, total[ROWS:], total[:ROWS])
    text_total = jnp.where(is_low, total[:ROWS], total[ROWS:])
    ysend_t[...] = jnp.concatenate([for_other, pad_rows]).astype(bf16)
    start("ty", ysend_t, yrecv_t, other_yhi)

    arrived("gr", gp_block(left_x, core))
    start("gfr", gp_block(left_x, core, 0, HEAD), gp_block(left_x, core, 0, HEAD), at_x(1))
    start("gs1", gp_block(left_x, core), gp_block(left_x, core), sibling)
    arrived("gl", gp_block(right_x, core))
    start(
        "gfl", gp_block(right_x, core, HEAD, tail_rows), gp_block(right_x, core, HEAD, tail_rows), at_x(-1)
    )
    start("gs2", gp_block(right_x, core), gp_block(right_x, core), sibling)

    arrived("ty", yrecv_t)
    text_total = text_total + yrecv_t[...].astype(f32)[:ROWS]
    tg_ref[...] = norm_backward(text_values, text_inverse, text_total).astype(bf16)

    arrived("gfr", gp_block(far_x, core, 0, HEAD))
    start("gs3", gp_block(far_x, core, 0, HEAD), gp_block(far_x, core, 0, HEAD), sibling)
    arrived("gfl", gp_block(far_x, core, HEAD, tail_rows))
    start(
        "gs4", gp_block(far_x, core, HEAD, tail_rows), gp_block(far_x, core, HEAD, tail_rows), sibling
    )
    arrived("gs0", gp_block(x, 1 - core))
    arrived("gs1", gp_block(left_x, 1 - core))
    arrived("gs2", gp_block(right_x, 1 - core))
    arrived("gs3", gp_block(far_x, 1 - core, 0, HEAD))
    arrived("gs4", gp_block(far_x, 1 - core, HEAD, tail_rows))

    part = jnp.dot(f_ref[...], gp[...], preferred_element_type=f32)
    ws[...] = jnp.concatenate([part, pad_rows]).astype(bf16)

    def piece_of(index):
        rows = pl.ds(pl.multiple_of((index // 3) * PIECE_ROWS, PIECE_ROWS), PIECE_ROWS)
        columns = pl.ds(pl.multiple_of((index % 3) * PIECE_COLS, PIECE_COLS), PIECE_COLS)
        return rows, columns

    def numbered(base, to, source, src, dst, target):
        return pltpu.make_async_remote_copy(
            src_ref=src, dst_ref=dst, send_sem=send_sem.at[base + to], recv_sem=recv_sem.at[base + source],
            device_id=target, device_id_type=MESH,
        )

    base = len(keys)
    again = base + 16

    def scatter(index):
        rows, columns = piece_of(index)
        return numbered(base, index, d, ws.at[rows, columns], wr.at[d], dp_at(index))

    def gather(index):
        return numbered(again, index, d, wa.at[d], wa.at[d], dp_at(index))

    for index in range(PIECES):
        @pl.when(d != index)
        def _(index=index):
            scatter(index).start()

    fg_ref[...] = lax.dot_general(
        w_ref[...], gp[...], (((1,), (1,)), ((), ())), preferred_element_type=f32
    ).astype(bf16)

    @pl.when(d < PIECES)
    def _():
        rows, columns = piece_of(d)
        wr[d] = ws[rows, columns]
        for source in range(16):
            @pl.when(d != source)
            def _(source=source):
                numbered(base, 0, source, wr.at[source], wr.at[source], sibling).wait_recv()
        total = wr[0].astype(f32)
        for source in range(1, 16):
            total = total + wr[source].astype(f32)
        wa[d] = total.astype(bf16)
        for index in range(16):
            @pl.when(d != index)
            def _(index=index):
                gather(index).start()

    for index in range(PIECES):
        @pl.when(d != index)
        def _(index=index):
            numbered(again, 0, index, wa.at[index], wa.at[index], sibling).wait_recv()
    for index in range(PIECES):
        first = (index // 3) * PIECE_ROWS
        count = min(PIECE_ROWS, ROWS - first)
        columns = pl.ds((index % 3) * PIECE_COLS, PIECE_COLS)
        pg_ref[pl.ds(first, count), columns] = wa[index].astype(f32)[:count]

    for copy in sent:
        copy.wait_send()

    @pl.when(jnp.logical_not(owner))
    def _():
        to_owner.wait_send()

    @pl.when(owner)
    def _():
        from_owner.wait_send()

    for index in range(PIECES):
        @pl.when(d != index)
        def _(index=index):
            scatter(index).wait_send()

    @pl.when(d < PIECES)
    def _():
        for index in range(16):
            @pl.when(d != index)
            def _(index=index):
                gather(index).wait_send()


def local(image_features, proj_weight, text_embed, text_match, logit_scale, logit_bias):
    vmem = pl.BlockSpec(memory_space=pltpu.VMEM)
    smem = pl.BlockSpec(memory_space=pltpu.SMEM)
    block = (BLOCK, EMBED)
    square = (GROUP, EMBED)
    tail = BLOCK - HEAD
    scratch = [
        pltpu.VMEM((PAD, EMBED), bf16),
        pltpu.VMEM((PAD, EMBED), bf16),
        pltpu.VMEM((2,) + square, bf16),
        pltpu.VMEM((PAD, EMBED), bf16),
        pltpu.VMEM((PAD, EMBED), bf16),
        pltpu.VMEM((8, 128), jnp.int32),
        pltpu.VMEM((8, 128), jnp.int32),
        pltpu.VMEM(square, bf16),
        pltpu.VMEM((8, 8, 128), jnp.int32),
        pltpu.VMEM((2, GROUP, 128), jnp.int32),
        pltpu.VMEM(square, f32),
        pltpu.VMEM(square, bf16),
        pltpu.VMEM((CHUNK, GROUP), f32),
        pltpu.VMEM(square, bf16),
        pltpu.VMEM(square, f32),
        pltpu.VMEM(square, f32),
        pltpu.VMEM((8,) + block, bf16),
        pltpu.VMEM((HEAD, EMBED), bf16),
        pltpu.VMEM((tail, EMBED), bf16),
        pltpu.VMEM((3,) + block, bf16),
        pltpu.VMEM((3,) + block, bf16),
        pltpu.VMEM((PAD, EMBED), bf16),
        pltpu.VMEM((PAD, EMBED), bf16),
        pltpu.VMEM((4,) + block, bf16),
        pltpu.VMEM((4,) + block, bf16),
        pltpu.VMEM((3,) + block, bf16),
        pltpu.VMEM((HEAD, EMBED), bf16),
        pltpu.VMEM((tail, EMBED), bf16),
        pltpu.VMEM(block, bf16),
        pltpu.VMEM(block, bf16),
        pltpu.VMEM(block, bf16),
        pltpu.VMEM(block, bf16),
        pltpu.VMEM(square, bf16),
        pltpu.VMEM((PAD, EMBED), bf16),
        pltpu.VMEM((16, PIECE_ROWS, PIECE_COLS), bf16),
        pltpu.VMEM((16, PIECE_ROWS, PIECE_COLS), bf16),
        pltpu.SemaphoreType.DMA((SEMS,)),
        pltpu.SemaphoreType.DMA((SEMS,)),
    ]
    rows = text_embed.shape[0]
    return pl.pallas_call(
        kernel,
        out_shape=(
            jax.ShapeDtypeStruct((rows, EMBED), bf16),
            jax.ShapeDtypeStruct((rows, GROUP), bf16),
            jax.ShapeDtypeStruct((rows, EMBED), f32),
        ),
        in_specs=[smem, smem, vmem, vmem, vmem, vmem],
        out_specs=(vmem, vmem, vmem),
        scratch_shapes=scratch,
        compiler_params=pltpu.CompilerParams(
            collective_id=0, has_side_effects=True, vmem_limit_bytes=60 * 1024 * 1024
        ),
        cost_estimate=pl.CostEstimate(flops=13_000_000_000, bytes_accessed=1_500_000, transcendentals=2_700_000),
    )(logit_scale, logit_bias, image_features, proj_weight, text_embed, text_match.reshape(1, rows))


def solution(mesh):
    return jax.shard_map(
        local,
        mesh=mesh,
        in_specs=(P("mp", "dp"), P("mp", None), P(("dp", "mp"), None), P(("dp", "mp")), P(), P()),
        out_specs=(P(("dp", "mp"), None), P("mp", "dp"), P("mp", None)),
        check_vma=False,
    )
```

time: 725 us -> 139 us (0.19)
  the two profiles are of different devices: /device:TPU:32 before, /device:TPU:24 now
where the time goes in v1:
time: 139 us
  Pallas kernels  134 us (96%)
  local copies, waits for them, and re-layouts  3.05 us (2%)
  between operations  1.95 us (1%)
    pallas_call x1, Pallas kernels, local(): pl.pallas_call(kernel, out_shape=(jax.ShapeDtypeStruct((rows, EMBED), bf1...  134 us
    unnamed x7, local copies, waits for them, and re-layouts  3.05 us

profile of v1, /device:TPU:24, one launch (start us, length us, event | category | flops | bytes accessed | tf_op | source)
XLA Modules:
  0.0 138.8 jit_solution(864567186965011413)
XLA Ops:
  1.9 133.8 %shard_map.85 = (bf16[72,1152]{1,0:T(8,128)(2,1)}, bf16[72,1152]{1,0:T(8,128)(2,1)}, f32[72,1152]{1,0:T(8,128)}) custom-call(f32[1]{0:T(128)S(6)} %copy.12.scale_ref, f32[1]{0:T(128)S(6)} %copy.13.bias_ref, bf16[72,1152]{1,0:T(8,128)(2,1)} %f_ref.1, bf16[72,1152]{1,0:T(8,128)(2,1)} %w_ref.1, bf16[72,1152]{1,0:T(8,128)(2,1)} %t_ref.1, s32[1,72]{1,0:T(1,128)} %bitcast.1), custom_call_target="tpu_custom_call" | custom-call | flops 12999999488 | bytes 1500000 | tf_op jit(solution)/shard_map/pallas_call | solution.py:535
  135.7 0.0 copy-start.1
  135.7 0.0 copy-start
  135.7 1.7 %copy.14 = bf16[72,1152]{1,0:T(8,128)(2,1)} copy(bf16[72,1152]{1,0:T(8,128)(2,1)} %get-tuple-element.6) | data formatting | bytes 331776
  137.4 0.0 copy-done.1
  137.4 0.7 copy.15
  138.0 0.0 copy-done
  138.0 0.7 copy.16
Async XLA Ops:
  135.7 1.7 %copy-start.1 = (bf16[72,1152]{1,0:T(8,128)(2,1)S(1)}, bf16[72,1152]{1,0:T(8,128)(2,1)}, u32[]{:S(2)}) copy-start(bf16[72,1152]{1,0:T(8,128)(2,1)} %get-tuple-element.7) | copy-start | bytes 497668
  135.7 2.3 %copy-start = (f32[72,1152]{1,0:T(8,128)S(1)}, f32[72,1152]{1,0:T(8,128)}, u32[]{:S(2)}) copy-start(f32[72,1152]{1,0:T(8,128)} %get-tuple-element.8) | copy-start | bytes 995332

commit v2 on v1

v2 whole, which is shorter than its diff:
```python
import functools

import jax
import jax.numpy as jnp
from jax import lax
from jax.experimental import pallas as pl
from jax.experimental.pallas import tpu as pltpu
from jax.sharding import PartitionSpec as P

MESH = pl.DeviceIdType.MESH
norm_floor = 1e-06
f32, bf16 = jnp.float32, jnp.bfloat16

ZS, XS = 8, 4
ROWS = 72
PAD = 80
BLOCK = 144
HEAD = 80
NEAR = 64
GROUP = 1152
EMBED = 1152
CHUNK = 288
TILE = 384
TEXT_ORDER = (0, -1, 1, -2, 2, -3, 3, 4)
TEXT_POS = {step: at for at, step in enumerate(TEXT_ORDER)}
IMAGE_ORDER = (2, 1, 3, 0)
PIECES, PIECE_ROWS, PIECE_COLS = 15, 16, 384
SEMS = 160


def inverse_norm(values):
    return lax.rsqrt(jnp.sum(values * values, axis=1, keepdims=True) + norm_floor)


def norm_backward(values, inverse, upstream):
    along = jnp.sum(values * upstream, axis=1, keepdims=True)
    return inverse * upstream - inverse * inverse * inverse * along * values


def kernel(
    scale_ref, bias_ref, f_ref, w_ref, t_ref, m_ref,
    tg_ref, fg_ref, pg_ref,
    xsend, xrecv, fw, tsend, trecv, msend, mrecv, tn, mt, mcol, proj, unit, logits, coef, dt, du,
    tout, tra, tlb, tr, tl, ysend_t, yrecv_t,
    csend, crecv, xout, xra, xlb, xr, xl, yout, yin, mine_sum, gp,
    ws, wr, wa,
    send_sem, recv_sem,
):
    d, m = lax.axis_index("dp"), lax.axis_index("mp")
    z, yhi = d // 2, d % 2
    x, ylo, core = m // 4, (m // 2) % 2, m % 2

    def at_z(step):
        return {"dp": lax.rem(z + step + ZS, ZS) * 2 + yhi, "mp": m}

    def at_x(step):
        return {"dp": d, "mp": lax.rem(x + step + XS, XS) * 4 + ylo * 2 + core}

    other_yhi = {"dp": z * 2 + (1 - yhi), "mp": m}
    other_ylo = {"dp": d, "mp": x * 4 + (1 - ylo) * 2 + core}
    sibling = {"dp": d, "mp": x * 4 + ylo * 2 + (1 - core)}

    def dp_at(index):
        return {"dp": index, "mp": m}

    barrier = pltpu.get_barrier_semaphore()
    partners = [sibling, other_ylo, other_yhi, at_x(1), at_x(-1), at_z(1), at_z(-1)]
    for partner in partners:
        pl.semaphore_signal(barrier, inc=1, device_id=partner, device_id_type=MESH)

    keys = {}

    def key(name):
        return keys.setdefault(name, len(keys))

    def describe(name, src, dst, target):
        k = key(name)
        return pltpu.make_async_remote_copy(
            src_ref=src, dst_ref=dst, send_sem=send_sem.at[k], recv_sem=recv_sem.at[k],
            device_id=target, device_id_type=MESH,
        )

    sent = []

    def start(name, src, dst, target):
        copy = describe(name, src, dst, target)
        copy.start()
        sent.append(copy)

    def arrived(name, dst, target=sibling):
        describe(name, dst, dst, target).wait_recv()

    f_mine, w_mine = f_ref[...].astype(f32), w_ref[...].astype(f32)
    is_first = core == 0
    pad_rows = jnp.zeros((PAD - ROWS, EMBED), f32)
    xsend[...] = jnp.concatenate([jnp.where(is_first, w_mine, f_mine), pad_rows]).astype(bf16)
    text_values = t_ref[...].astype(f32)
    text_inverse = inverse_norm(text_values)
    text_mine = text_values * text_inverse
    tsend[...] = jnp.concatenate([text_mine, pad_rows]).astype(bf16)
    msend[...] = jnp.zeros_like(msend)
    msend[0:1, 0:ROWS] = m_ref[...]
    pl.semaphore_wait(barrier, len(partners))

    start("x0", xsend, xrecv, sibling)

    def text_rows(step, part):
        first = TEXT_POS[step] * BLOCK
        return pl.ds(first, NEAR) if part == 0 else pl.ds(first + NEAR, BLOCK - NEAR)

    def text_forward(step, part, way, new_step):
        start(("t", new_step, part), tn.at[text_rows(step, part)], tn.at[text_rows(new_step, part)], at_z(way))
        if part == 1:
            start(("m", new_step), mt.at[TEXT_POS[step]], mt.at[TEXT_POS[new_step]], at_z(way))

    def text_arrived(step, part):
        arrived(("t", step, part), tn.at[text_rows(step, part)])
        if part == 1:
            arrived(("m", step), mt.at[TEXT_POS[step]])

    tn[pl.ds(0, NEAR), :] = text_mine[:NEAR].astype(bf16)
    text_forward(0, 0, 1, -1)
    text_forward(0, 0, -1, 1)
    start("t0", tsend, trecv, other_yhi)
    start("m0", msend, mrecv, other_yhi)

    def slot(index, count=1):
        return pl.ds(index * BLOCK, count * BLOCK)

    def mine(index):
        return fw.at[core, slot(index)]

    def share(index):
        start(("fs", index), mine(index), mine(index), sibling)

    own = jnp.where(is_first, f_mine, w_mine)
    arrived("x0", xrecv)
    theirs = xrecv[...].astype(f32)[:ROWS]
    fw[core, slot(0), :] = jnp.concatenate(
        [jnp.where(is_first, own, theirs), jnp.where(is_first, theirs, own)]
    ).astype(bf16)
    start(("fx", 1), mine(0), mine(1), other_ylo)
    start(("fx", 4), mine(0), mine(4), at_x(1))
    start(("fx", 2), mine(0), mine(2), at_x(-1))
    share(0)

    arrived("t0", trecv)
    arrived("m0", mrecv)
    theirs = trecv[...].astype(f32)[:ROWS]
    tn[text_rows(0, 1), :] = jnp.concatenate([tsend[...].astype(f32)[NEAR:ROWS], theirs]).astype(bf16)
    mt[0, 0:1, :] = msend[0:1, :]
    mt[0, 1:2, :] = mrecv[0:1, :]
    mt[0, 2:8, :] = jnp.zeros((6, 128), jnp.int32)
    text_forward(0, 1, 1, -1)
    text_forward(0, 1, -1, 1)

    def text_pass(step, part):
        for way in (1, -1):
            text_arrived(-way * step, part)
            text_forward(-way * step, part, way, -way * (step + 1))

    text_pass(1, 0)
    arrived(("fx", 1), mine(1))
    start(("fx", 5), mine(1), mine(5), at_x(1))
    start(("fx", 3), mine(1), mine(3), at_x(-1))
    share(1)
    arrived(("fx", 4), mine(4))
    start(("fx", 6), mine(4), mine(6), at_x(1))
    share(4)
    arrived(("fx", 2), mine(2))
    share(2)
    text_pass(1, 1)
    text_pass(2, 0)
    arrived(("fx", 3), mine(3))
    start(("fx", 7), mine(3), mine(7), at_x(-1))
    share(3)
    arrived(("fx", 5), mine(5))
    share(5)
    text_pass(2, 1)
    text_arrived(-3, 0)
    text_forward(-3, 0, 1, 4)
    arrived(("fx", 6), mine(6))
    share(6)
    arrived(("fx", 7), mine(7))
    share(7)
    text_arrived(3, 0)
    text_arrived(3, 1)
    text_forward(3, 1, -1, 4)
    for index in range(8):
        arrived(("fs", index), fw.at[1 - core, slot(index)])

    def project(tile, _):
        columns = pl.ds(pl.multiple_of(tile * TILE, TILE), TILE)
        values = lax.dot_general(
            fw[0, :, columns], fw[1], (((0,), (0,)), ((), ())), preferred_element_type=f32
        )
        normal = (values * inverse_norm(values)).astype(bf16)
        for part in range(TILE // 96):
            piece = tile * (TILE // 96) + part
            away = lax.rem(piece // 3 - x + XS, XS)
            place = jnp.where(away == 2, 0, jnp.where(away == 1, 1, jnp.where(away == 3, 2, 3)))
            row = pl.multiple_of(place * CHUNK + (piece % 3) * 96, 96)
            proj[pl.ds(row, 96), :] = values[part * 96:(part + 1) * 96]
            unit[pl.ds(row, 96), :] = normal[part * 96:(part + 1) * 96]
        return 0

    lax.fori_loop(0, GROUP // TILE, project, 0)

    lane = lax.broadcasted_iota(jnp.int32, (1, GROUP), 1)
    image_index = jnp.zeros_like(lane)
    for place, away in enumerate(IMAGE_ORDER):
        base = d * GROUP + lax.rem(x + away, XS) * CHUNK - place * CHUNK
        image_index = jnp.where(lane // CHUNK == place, base + lane, image_index)

    row_number = lax.broadcasted_iota(jnp.int32, (ROWS, 128), 0)

    def columns_of(step):
        place = TEXT_POS[step]
        from_z = lax.rem(z + step + ZS, ZS)
        for which, high in enumerate((yhi, 1 - yhi)):
            row = mt[place, which:which + 1, :]
            column = jnp.transpose(jnp.broadcast_to(row, (128, 128)))[:ROWS]
            rows = pl.ds(place * BLOCK + which * ROWS, ROWS)
            mcol[0, rows, :] = column
            mcol[1, rows, :] = ((from_z * 2 + high) * 16 + m) * ROWS + row_number

    log2e = 1.4426950408889634
    scaling = scale_ref[0]
    slope, shift = scaling * log2e, bias_ref[0] * log2e

    def coefficients_of(chunk):
        for step in TEXT_ORDER[2 * chunk:2 * chunk + 2]:
            columns_of(step)
        rows = pl.ds(chunk * CHUNK, CHUNK)
        logits[...] = lax.dot_general(
            tn[rows, :], unit[...], (((1,), (1,)), ((), ())), preferred_element_type=f32
        )

        def coefficients(step, _):
            at = pl.multiple_of(step * 16, 16)
            here = pl.ds(chunk * CHUNK + at, 16)
            match = mcol[0, here, 0:1]
            index = mcol[1, here, 0:1]
            positive = (index == image_index) | (match == image_index)
            power = slope * logits[pl.ds(at, 16), :] + shift
            grown = 1.0 + jnp.exp2(jnp.where(positive, power, -power))
            coef[here, :] = (
                jnp.where(positive, -scaling, scaling) * pl.reciprocal(grown, approx=True)
            ).astype(bf16)
            return 0

        lax.fori_loop(0, CHUNK // 16, coefficients, 0)

    coefficients_of(0)
    coefficients_of(1)
    text_arrived(-3, 1)
    coefficients_of(2)
    text_arrived(4, 0)
    text_arrived(4, 1)
    coefficients_of(3)

    parts = ((0, HEAD), (HEAD, BLOCK - HEAD))

    def image_tile(tile):
        columns = pl.ds(tile * TILE, TILE)
        du[columns, :] = lax.dot_general(
            coef[:, columns], tn[...], (((0,), (0,)), ((), ())), preferred_element_type=f32
        )

    def text_tile(chunk):
        rows = pl.ds(chunk * CHUNK, CHUNK)
        dt[rows, :] = jnp.dot(coef[rows, :], unit[...], preferred_element_type=f32)

    def image_block(place, which, first=0, count=BLOCK):
        return pl.ds(pl.multiple_of(place * CHUNK + which * BLOCK + first, 16), count)

    def to_sibling(place):
        csend[place] = du[image_block(place, 1 - core), :].astype(bf16)
        start(("c", place), csend.at[place], crecv.at[place], sibling)

    def with_sibling(place, part):
        first, count = parts[part]
        return du[image_block(place, core, first, count), :] + crecv[place, pl.ds(first, count), :].astype(f32)

    def image_send(place, part, way, buffer, extra=None):
        first, count = parts[part]
        values = with_sibling(place, part)
        if extra is not None:
            values = values + extra
        xout[place, pl.ds(first, count), :] = values.astype(bf16)
        there = buffer.at[pl.ds(first, count)] if buffer.shape[0] == BLOCK else buffer
        start(("x", place, part, way), xout.at[place, pl.ds(first, count)], there, at_x(way))

    def image_arrived(place, part, way, buffer):
        first, count = parts[part]
        there = buffer.at[pl.ds(first, count)] if buffer.shape[0] == BLOCK else buffer
        arrived(("x", place, part, way), there)
        return there[...].astype(f32)

    def text_partial(step, part):
        first, count = parts[part]
        return dt[pl.ds(TEXT_POS[step] * BLOCK + first, count), :]

    def text_buffer(way, away, part):
        first, count = parts[part]
        if away == 4:
            return tra if way == 1 else tlb
        return (tr if way == 1 else tl).at[3 - away, pl.ds(first, count)]

    def text_came(way, away, part):
        there = text_buffer(way, away, part)
        arrived(("ts", way, away, part), there)
        return there[...].astype(f32)

    def text_send(way, away, part):
        first, count = parts[part]
        step = 4 if away == 4 else way * away
        values = text_partial(step, part)
        if away == 2 or away == 1 or (away == 3 and part == (0 if way == 1 else 1)):
            values = values + text_came(way, away + 1, part)
        place = TEXT_POS[step]
        tout[place, pl.ds(first, count), :] = values.astype(bf16)
        start(
            ("ts", way, away, part), tout.at[place, pl.ds(first, count)], text_buffer(way, away, part), at_z(way)
        )

    image_tile(0)
    to_sibling(0)
    image_tile(1)
    to_sibling(1)
    arrived(("c", 0), crecv.at[0])
    image_send(0, 0, 1, xra)
    image_send(0, 1, -1, xlb)
    image_tile(2)
    to_sibling(2)
    to_sibling(3)
    arrived(("c", 1), crecv.at[1])
    image_send(1, 1, 1, xr)
    text_tile(3)
    text_send(1, 4, 0)
    text_send(-1, 4, 1)
    arrived(("c", 2), crecv.at[2])
    image_send(2, 0, -1, xl)
    text_send(1, 3, 1)
    text_tile(2)
    text_send(-1, 3, 0)
    image_send(1, 0, 1, xr, image_arrived(0, 0, 1, xra))
    image_send(2, 1, -1, xl, image_arrived(0, 1, -1, xlb))
    text_tile(1)
    text_tile(0)
    text_send(1, 3, 0)
    text_send(-1, 3, 1)
    arrived(("c", 3), crecv.at[3])

    def gp_block(from_x, which, part=None):
        first, count = (0, BLOCK) if part is None else parts[part]
        return gp.at[pl.ds(pl.multiple_of(from_x * CHUNK + which * BLOCK + first, 16), count)]

    owner = ylo == core
    not_owner = jnp.logical_not(owner)
    text_send(1, 2, 1)
    text_send(-1, 2, 0)

    def to_owner(part):
        rows = pl.ds(*parts[part])
        return describe(("yo", part), yout.at[rows], yin.at[rows], other_ylo)

    def from_owner(part):
        block = gp_block(x, core, part)
        return describe(("yg", part), block, block, other_ylo)

    for part in range(2):
        rows = pl.ds(*parts[part])
        mine_sum[rows, :] = (
            with_sibling(3, part) + image_arrived(1, part, 1, xr) + image_arrived(2, part, -1, xl)
        )

        @pl.when(not_owner)
        def _(rows=rows, part=part):
            yout[rows, :] = mine_sum[rows, :].astype(bf16)
            to_owner(part).start()

    text_send(1, 2, 0)
    text_send(-1, 2, 1)

    for part in range(2):
        @pl.when(owner)
        def _(part=part):
            first, count = parts[part]
            to_owner(part).wait_recv()
            total = mine_sum[pl.ds(first, count), :] + yin[pl.ds(first, count), :].astype(f32)
            projected = proj[image_block(3, core, first, count), :]
            place = pl.multiple_of(x * CHUNK + core * BLOCK + first, 16)
            gp[pl.ds(place, count), :] = norm_backward(
                projected, inverse_norm(projected), total
            ).astype(bf16)
            from_owner(part).start()

        @pl.when(not_owner)
        def _(part=part):
            from_owner(part).wait_recv()

        block = gp_block(x, core, part)
        start(("gr", part), block, block, at_x(1))
        start(("gl", part), block, block, at_x(-1))
        start(("gs", 0, part), block, block, sibling)

    left_x, right_x, far_x = lax.rem(x + 3, XS), lax.rem(x + 1, XS), lax.rem(x + 2, XS)

    def gp_share(index, from_x, part):
        block = gp_block(from_x, core, part)
        start(("gs", index, part), block, block, sibling)

    text_send(1, 1, 1)
    text_send(-1, 1, 0)
    block = gp_block(left_x, core, 0)
    arrived(("gr", 0), block)
    start("gfr", block, block, at_x(1))
    gp_share(1, left_x, 0)
    arrived(("gl", 0), gp_block(right_x, core, 0))
    gp_share(2, right_x, 0)
    block = gp_block(right_x, core, 1)
    arrived(("gl", 1), block)
    start("gfl", block, block, at_x(-1))
    gp_share(2, right_x, 1)
    arrived(("gr", 1), gp_block(left_x, core, 1))
    gp_share(1, left_x, 1)
    text_send(1, 1, 0)
    text_send(-1, 1, 1)
    arrived("gfr", gp_block(far_x, core, 0))
    gp_share(3, far_x, 0)
    arrived("gfl", gp_block(far_x, core, 1))
    gp_share(3, far_x, 1)

    total = jnp.concatenate(
        [text_partial(0, part) + text_came(1, 1, part) + text_came(-1, 1, part) for part in range(2)]
    )
    ysend_t[...] = jnp.concatenate([total[ROWS:], pad_rows]).astype(bf16)
    start("ty", ysend_t, yrecv_t, other_yhi)

    for part in range(2):
        for index, from_x in enumerate((x, left_x, right_x, far_x)):
            arrived(("gs", index, part), gp_block(from_x, 1 - core, part))

    part = jnp.dot(f_ref[...], gp[...], preferred_element_type=f32)
    ws[...] = jnp.concatenate([part, pad_rows]).astype(bf16)

    def piece_of(index):
        rows = pl.ds(pl.multiple_of((index // 3) * PIECE_ROWS, PIECE_ROWS), PIECE_ROWS)
        columns = pl.ds(pl.multiple_of((index % 3) * PIECE_COLS, PIECE_COLS), PIECE_COLS)
        return rows, columns

    def numbered(base, to, source, src, dst, target):
        return pltpu.make_async_remote_copy(
            src_ref=src, dst_ref=dst, send_sem=send_sem.at[base + to], recv_sem=recv_sem.at[base + source],
            device_id=target, device_id_type=MESH,
        )

    base = len(keys)
    again = base + 16

    def scatter(index):
        rows, columns = piece_of(index)
        return numbered(base, index, d, ws.at[rows, columns], wr.at[d], dp_at(index))

    def gather(index):
        return numbered(again, index, d, wa.at[d], wa.at[d], dp_at(index))

    for index in range(PIECES):
        @pl.when(d != index)
        def _(index=index):
            scatter(index).start()

    fg_ref[...] = lax.dot_general(
        w_ref[...], gp[...], (((1,), (1,)), ((), ())), preferred_element_type=f32
    ).astype(bf16)

    arrived("ty", yrecv_t)
    text_total = total[:ROWS] + yrecv_t[...].astype(f32)[:ROWS]
    tg_ref[...] = norm_backward(text_values, text_inverse, text_total).astype(bf16)

    @pl.when(d < PIECES)
    def _():
        rows, columns = piece_of(d)
        wr[d] = ws[rows, columns]
        for source in range(16):
            @pl.when(d != source)
            def _(source=source):
                numbered(base, 0, source, wr.at[source], wr.at[source], sibling).wait_recv()
        total = wr[0].astype(f32)
        for source in range(1, 16):
            total = total + wr[source].astype(f32)
        wa[d] = total.astype(bf16)
        for index in range(16):
            @pl.when(d != index)
            def _(index=index):
                gather(index).start()

    for index in range(PIECES):
        @pl.when(d != index)
        def _(index=index):
            numbered(again, 0, index, wa.at[index], wa.at[index], sibling).wait_recv()
    for index in range(PIECES):
        first = (index // 3) * PIECE_ROWS
        count = min(PIECE_ROWS, ROWS - first)
        columns = pl.ds((index % 3) * PIECE_COLS, PIECE_COLS)
        pg_ref[pl.ds(first, count), columns] = wa[index].astype(f32)[:count]

    for copy in sent:
        copy.wait_send()

    @pl.when(not_owner)
    def _():
        for part in range(2):
            to_owner(part).wait_send()

    @pl.when(owner)
    def _():
        for part in range(2):
            from_owner(part).wait_send()

    for index in range(PIECES):
        @pl.when(d != index)
        def _(index=index):
            scatter(index).wait_send()

    @pl.when(d < PIECES)
    def _():
        for index in range(16):
            @pl.when(d != index)
            def _(index=index):
                gather(index).wait_send()


def local(image_features, proj_weight, text_embed, text_match, logit_scale, logit_bias):
    vmem = pl.BlockSpec(memory_space=pltpu.VMEM)
    smem = pl.BlockSpec(memory_space=pltpu.SMEM)
    block = (BLOCK, EMBED)
    square = (GROUP, EMBED)
    tail = BLOCK - HEAD
    scratch = [
        pltpu.VMEM((PAD, EMBED), bf16),
        pltpu.VMEM((PAD, EMBED), bf16),
        pltpu.VMEM((2,) + square, bf16),
        pltpu.VMEM((PAD, EMBED), bf16),
        pltpu.VMEM((PAD, EMBED), bf16),
        pltpu.VMEM((8, 128), jnp.int32),
        pltpu.VMEM((8, 128), jnp.int32),
        pltpu.VMEM(square, bf16),
        pltpu.VMEM((8, 8, 128), jnp.int32),
        pltpu.VMEM((2, GROUP, 128), jnp.int32),
        pltpu.VMEM(square, f32),
        pltpu.VMEM(square, bf16),
        pltpu.VMEM((CHUNK, GROUP), f32),
        pltpu.VMEM(square, bf16),
        pltpu.VMEM(square, f32),
        pltpu.VMEM(square, f32),
        pltpu.VMEM((8,) + block, bf16),
        pltpu.VMEM((HEAD, EMBED), bf16),
        pltpu.VMEM((tail, EMBED), bf16),
        pltpu.VMEM((3,) + block, bf16),
        pltpu.VMEM((3,) + block, bf16),
        pltpu.VMEM((PAD, EMBED), bf16),
        pltpu.VMEM((PAD, EMBED), bf16),
        pltpu.VMEM((4,) + block, bf16),
        pltpu.VMEM((4,) + block, bf16),
        pltpu.VMEM((3,) + block, bf16),
        pltpu.VMEM((HEAD, EMBED), bf16),
        pltpu.VMEM((tail, EMBED), bf16),
        pltpu.VMEM(block, bf16),
        pltpu.VMEM(block, bf16),
        pltpu.VMEM(block, bf16),
        pltpu.VMEM(block, bf16),
        pltpu.VMEM(block, f32),
        pltpu.VMEM(square, bf16),
        pltpu.VMEM((PAD, EMBED), bf16),
        pltpu.VMEM((16, PIECE_ROWS, PIECE_COLS), bf16),
        pltpu.VMEM((16, PIECE_ROWS, PIECE_COLS), bf16),
        pltpu.SemaphoreType.DMA((SEMS,)),
        pltpu.SemaphoreType.DMA((SEMS,)),
    ]
    rows = text_embed.shape[0]
    return pl.pallas_call(
        kernel,
        out_shape=(
            jax.ShapeDtypeStruct((rows, EMBED), bf16),
            jax.ShapeDtypeStruct((rows, GROUP), bf16),
            jax.ShapeDtypeStruct((rows, EMBED), f32),
        ),
        in_specs=[smem, smem, vmem, vmem, vmem, vmem],
        out_specs=(vmem, vmem, vmem),
        scratch_shapes=scratch,
        compiler_params=pltpu.CompilerParams(
            collective_id=0, has_side_effects=True, vmem_limit_bytes=60 * 1024 * 1024
        ),
        cost_estimate=pl.CostEstimate(flops=13_000_000_000, bytes_accessed=1_500_000, transcendentals=2_700_000),
    )(logit_scale, logit_bias, image_features, proj_weight, text_embed, text_match.reshape(1, rows))


def solution(mesh):
    return jax.shard_map(
        local,
        mesh=mesh,
        in_specs=(P("mp", "dp"), P("mp", None), P(("dp", "mp"), None), P(("dp", "mp")), P(), P()),
        out_specs=(P(("dp", "mp"), None), P("mp", "dp"), P("mp", None)),
        check_vma=False,
    )
```

time: 139 us -> 119 us (0.86)
  the two profiles are of different devices: /device:TPU:24 before, /device:TPU:32 now
where the time goes in v2:
time: 119 us; the launch traced here: 117 us
  Pallas kernels  112 us (94%)
  local copies, waits for them, and re-layouts  3.05 us (3%)
  between operations  1.95 us (2%)
    pallas_call x1, Pallas kernels, local(): pl.pallas_call(kernel, out_shape=(jax.ShapeDtypeStruct((rows, EMBED), bf1...  112 us
    unnamed x7, local copies, waits for them, and re-layouts  3.05 us

profile of v2, /device:TPU:32, one launch (start us, length us, event | category | flops | bytes accessed | tf_op | source)
XLA Modules:
  0.0 116.5 jit_solution(765708270073191586)
XLA Ops:
  1.9 111.5 %shard_map.85 = (bf16[72,1152]{1,0:T(8,128)(2,1)}, bf16[72,1152]{1,0:T(8,128)(2,1)}, f32[72,1152]{1,0:T(8,128)}) custom-call(f32[1]{0:T(128)S(6)} %copy.12.scale_ref, f32[1]{0:T(128)S(6)} %copy.13.bias_ref, bf16[72,1152]{1,0:T(8,128)(2,1)} %f_ref.1, bf16[72,1152]{1,0:T(8,128)(2,1)} %w_ref.1, bf16[72,1152]{1,0:T(8,128)(2,1)} %t_ref.1, s32[1,72]{1,0:T(1,128)} %bitcast.1), custom_call_target="tpu_custom_call" | custom-call | flops 12999999488 | bytes 1500000 | tf_op jit(solution)/shard_map/pallas_call | solution.py:583
  113.4 0.0 copy-start.1
  113.5 0.0 copy-start
  113.5 1.7 %copy.14 = bf16[72,1152]{1,0:T(8,128)(2,1)} copy(bf16[72,1152]{1,0:T(8,128)(2,1)} %get-tuple-element.6) | data formatting | bytes 331776
  115.1 0.0 copy-done.1
  115.1 0.7 copy.15
  115.8 0.0 copy-done
  115.8 0.7 copy.16
Async XLA Ops:
  113.4 1.7 %copy-start.1 = (bf16[72,1152]{1,0:T(8,128)(2,1)S(1)}, bf16[72,1152]{1,0:T(8,128)(2,1)}, u32[]{:S(2)}) copy-start(bf16[72,1152]{1,0:T(8,128)(2,1)} %get-tuple-element.7) | copy-start | bytes 497668
  113.5 2.3 %copy-start = (f32[72,1152]{1,0:T(8,128)S(1)}, f32[72,1152]{1,0:T(8,128)}, u32[]{:S(2)}) copy-start(f32[72,1152]{1,0:T(8,128)} %get-tuple-element.8) | copy-start | bytes 995332

commit v3 on v2

--- a/solution.py
+++ b/solution.py
@@ -23,9 +23,8 @@
 TILE = 384
 TEXT_ORDER = (0, -1, 1, -2, 2, -3, 3, 4)
 TEXT_POS = {step: at for at, step in enumerate(TEXT_ORDER)}
-IMAGE_ORDER = (2, 1, 3, 0)
 PIECES, PIECE_ROWS, PIECE_COLS = 15, 16, 384
-SEMS = 160
+SEMS = 224
 
 
 def inverse_norm(values):
@@ -40,7 +39,7 @@
 def kernel(
     scale_ref, bias_ref, f_ref, w_ref, t_ref, m_ref,
     tg_ref, fg_ref, pg_ref,
-    xsend, xrecv, fw, tsend, trecv, msend, mrecv, tn, mt, mcol, proj, unit, logits, coef, dt, du,
+    xsend, xrecv, wf, ff, tsend, trecv, msend, mrecv, tn, mt, mcol, proj, unit, logits, coef, dt, du,
     tout, tra, tlb, tr, tl, ysend_t, yrecv_t,
     csend, crecv, xout, xra, xlb, xr, xl, yout, yin, mine_sum, gp,
     ws, wr, wa,
@@ -53,8 +52,12 @@
     def at_z(step):
         return {"dp": lax.rem(z + step + ZS, ZS) * 2 + yhi, "mp": m}
 
-    def at_x(step):
-        return {"dp": d, "mp": lax.rem(x + step + XS, XS) * 4 + ylo * 2 + core}
+    beside_x = {
+        way: {"dp": d, "mp": lax.rem(x + way + XS, XS) * 4 + ylo * 2 + core} for way in (1, -1)
+    }
+
+    def at_x(way):
+        return beside_x[way]
 
     other_yhi = {"dp": z * 2 + (1 - yhi), "mp": m}
     other_ylo = {"dp": d, "mp": x * 4 + (1 - ylo) * 2 + core}
@@ -80,20 +83,25 @@
             device_id=target, device_id_type=MESH,
         )
 
-    sent = []
+    sent = {}
 
     def start(name, src, dst, target):
         copy = describe(name, src, dst, target)
         copy.start()
-        sent.append(copy)
+        sent[name] = lambda: copy
 
     def arrived(name, dst, target=sibling):
         describe(name, dst, dst, target).wait_recv()
 
     f_mine, w_mine = f_ref[...].astype(f32), w_ref[...].astype(f32)
     is_first = core == 0
+    owner = ylo == core
+    not_owner = jnp.logical_not(owner)
+    left_x, right_x, far_x = lax.rem(x + 3, XS), lax.rem(x + 1, XS), lax.rem(x + 2, XS)
+    parts = ((0, HEAD), (HEAD, BLOCK - HEAD))
     pad_rows = jnp.zeros((PAD - ROWS, EMBED), f32)
-    xsend[...] = jnp.concatenate([jnp.where(is_first, w_mine, f_mine), pad_rows]).astype(bf16)
+    xsend[0] = jnp.concatenate([w_mine, pad_rows]).astype(bf16)
+    xsend[1] = jnp.concatenate([f_mine, pad_rows]).astype(bf16)
     text_values = t_ref[...].astype(f32)
     text_inverse = inverse_norm(text_values)
     text_mine = text_values * text_inverse
@@ -124,26 +132,151 @@
     start("t0", tsend, trecv, other_yhi)
     start("m0", msend, mrecv, other_yhi)
 
-    def slot(index, count=1):
-        return pl.ds(index * BLOCK, count * BLOCK)
-
-    def mine(index):
-        return fw.at[core, slot(index)]
-
-    def share(index):
-        start(("fs", index), mine(index), mine(index), sibling)
-
-    own = jnp.where(is_first, f_mine, w_mine)
+    def block_rows(from_x, which, part=None):
+        first, count = (0, BLOCK) if part is None else parts[part]
+        return pl.ds(pl.multiple_of(from_x * CHUNK + which * BLOCK + first, 16), count)
+
+    def block_of(name, from_x, which, part=None):
+        rows = block_rows(from_x, which, part)
+        return wf.at[rows] if name == "w" else ff.at[:, rows]
+
+    def by_role(of_owner, of_other):
+        pl.when(owner)(of_owner)
+        pl.when(not_owner)(of_other)
+
+    def by_core(run):
+        for index in range(2):
+            pl.when(core == index)(functools.partial(run, index))
+
+    class Block:
+        def __init__(self, name, what, from_x, which, target, halves=False):
+            self.name, self.what, self.from_x, self.which = name, what, from_x, which
+            self.target, self.halves = target, halves
+
+        def describe(self, part=None, target=None):
+            block = block_of(self.what, self.from_x, self.which, part)
+            return describe(self.name, block, block, self.target if target is None else target)
+
+        def run(self, method, mine=True):
+            if self.halves:
+                by_core(lambda index: getattr(self.describe(index if mine else 1 - index), method)())
+            else:
+                getattr(self.describe(), method)()
+
+        def start(self):
+            self.run("start")
+            sent[self.name] = self
+
+        def arrive(self, mine=True):
+            self.run("wait_recv", mine)
+
+        def wait_send(self):
+            self.run("wait_send")
+
+    way_x = lax.rem(x + 1 + 2 * core, XS)
+    ahead = {"dp": d, "mp": way_x * 4 + ylo * 2 + core}
+    behind_x = lax.rem(x + 3 + 2 * core, XS)
+    other_behind_x = lax.rem(x + 1 + 2 * core, XS)
+    other_y = 1 - ylo
+
+    def w_pair(name, from_mine, from_theirs, which, target, halves):
+        return Block(name, "w", from_mine, which, target, halves), Block(name, "w", from_theirs[0], from_theirs[1], target, halves)
+
+    w_own, w_behind = w_pair("w1", x, (behind_x, ylo), ylo, ahead, False)
+    w_on, w_far = w_pair("w2", behind_x, (far_x, ylo), ylo, ahead, True)
+    y_own, y_own_in = w_pair("y0", x, (x, other_y), ylo, other_ylo, True)
+    y_behind, y_behind_in = w_pair("y1", behind_x, (behind_x, other_y), ylo, other_ylo, False)
+    y_far, y_far_in = w_pair("y2", far_x, (far_x, other_y), ylo, other_ylo, True)
+
+    def w_share(name, from_x, which, halves):
+        theirs = other_behind_x if not halves else from_x
+        return w_pair(name, from_x, (theirs, which), which, sibling, halves)
+
+    shares = {
+        "s1": w_share("s1", behind_x, ylo, False),
+        "s2": w_share("s2", far_x, ylo, True),
+        "s3": w_share("s3", x, other_y, True),
+        "s4": w_share("s4", behind_x, other_y, False),
+        "s5": w_share("s5", far_x, other_y, True),
+    }
+
+    def same(kind, name, from_x, target, part=None):
+        block = block_of(name, from_x, core, part)
+        return describe((kind, name, part), block, block, target)
+
+    def move(kind, name, from_x, target, part=None):
+        same(kind, name, from_x, target, part).start()
+        sent[(kind, name, part)] = functools.partial(same, kind, name, from_x, target, part)
+
+    def came(kind, name, from_x, part=None):
+        same(kind, name, from_x, sibling, part).wait_recv()
+
+    tiles = GROUP // TILE
+    gathered = ("f",)
+
+    def spread(name):
+        move("right", name, x, at_x(1))
+        move("left", name, x, at_x(-1))
+
+    def spread_other(name):
+        same("across", name, x, other_ylo).wait_recv()
+        spread(name)
+        same("share", name, x, sibling).start()
+
+    def far(name):
+        came("right", name, left_x)
+        move("far", name, left_x, at_x(1), 0)
+        move("share_left", name, left_x, sibling)
+        came("left", name, right_x)
+        move("far", name, right_x, at_x(-1), 1)
+        move("share_right", name, right_x, sibling)
+
+    def finish(name):
+        for part in range(2):
+            came("far", name, far_x, part)
+            move("share_far", name, far_x, sibling, part)
+
+    def complete(name):
+        for kind, from_x, part in (
+            ("share_left", left_x, None), ("share_right", right_x, None),
+            ("share_far", far_x, 0), ("share_far", far_x, 1),
+        ):
+            block = block_of(name, from_x, 1 - core, part)
+            describe((kind, name, part), block, block, sibling).wait_recv()
+
+        @pl.when(owner)
+        def _():
+            block = block_of(name, x, 1 - core)
+            describe(("share", name, None), block, block, sibling).wait_recv()
+
     arrived("x0", xrecv)
-    theirs = xrecv[...].astype(f32)[:ROWS]
-    fw[core, slot(0), :] = jnp.concatenate(
-        [jnp.where(is_first, own, theirs), jnp.where(is_first, theirs, own)]
-    ).astype(bf16)
-    start(("fx", 1), mine(0), mine(1), other_ylo)
-    start(("fx", 4), mine(0), mine(4), at_x(1))
-    start(("fx", 2), mine(0), mine(2), at_x(-1))
-    share(0)
-
+    for index, own in enumerate((w_mine, f_mine)):
+        theirs = xrecv[index].astype(f32)[:ROWS]
+        packed = jnp.concatenate(
+            [jnp.where(is_first, own, theirs), jnp.where(is_first, theirs, own)]
+        ).astype(bf16)
+        rows = block_rows(x, ylo)
+        if index == 0:
+            wf[rows, :] = packed
+        else:
+            for tile in range(tiles):
+                ff[tile, rows, :] = packed[:, tile * TILE:(tile + 1) * TILE]
+
+    w_own.start()
+
+    @pl.when(owner)
+    def _():
+        same("across", "f", x, other_ylo).start()
+        spread("f")
+
+    y_own.start()
+
+    def text_pass(step, part):
+        for way in (1, -1):
+            text_arrived(-way * step, part)
+            text_forward(-way * step, part, way, -way * (step + 1))
+
+    text_pass(1, 0)
     arrived("t0", trecv)
     arrived("m0", mrecv)
     theirs = trecv[...].astype(f32)[:ROWS]
@@ -154,64 +287,6 @@
     text_forward(0, 1, 1, -1)
     text_forward(0, 1, -1, 1)
 
-    def text_pass(step, part):
-        for way in (1, -1):
-            text_arrived(-way * step, part)
-            text_forward(-way * step, part, way, -way * (step + 1))
-
-    text_pass(1, 0)
-    arrived(("fx", 1), mine(1))
-    start(("fx", 5), mine(1), mine(5), at_x(1))
-    start(("fx", 3), mine(1), mine(3), at_x(-1))
-    share(1)
-    arrived(("fx", 4), mine(4))
-    start(("fx", 6), mine(4), mine(6), at_x(1))
-    share(4)
-    arrived(("fx", 2), mine(2))
-    share(2)
-    text_pass(1, 1)
-    text_pass(2, 0)
-    arrived(("fx", 3), mine(3))
-    start(("fx", 7), mine(3), mine(7), at_x(-1))
-    share(3)
-    arrived(("fx", 5), mine(5))
-    share(5)
-    text_pass(2, 1)
-    text_arrived(-3, 0)
-    text_forward(-3, 0, 1, 4)
-    arrived(("fx", 6), mine(6))
-    share(6)
-    arrived(("fx", 7), mine(7))
-    share(7)
-    text_arrived(3, 0)
-    text_arrived(3, 1)
-    text_forward(3, 1, -1, 4)
-    for index in range(8):
-        arrived(("fs", index), fw.at[1 - core, slot(index)])
-
-    def project(tile, _):
-        columns = pl.ds(pl.multiple_of(tile * TILE, TILE), TILE)
-        values = lax.dot_general(
-            fw[0, :, columns], fw[1], (((0,), (0,)), ((), ())), preferred_element_type=f32
-        )
-        normal = (values * inverse_norm(values)).astype(bf16)
-        for part in range(TILE // 96):
-            piece = tile * (TILE // 96) + part
-            away = lax.rem(piece // 3 - x + XS, XS)
-            place = jnp.where(away == 2, 0, jnp.where(away == 1, 1, jnp.where(away == 3, 2, 3)))
-            row = pl.multiple_of(place * CHUNK + (piece % 3) * 96, 96)
-            proj[pl.ds(row, 96), :] = values[part * 96:(part + 1) * 96]
-            unit[pl.ds(row, 96), :] = normal[part * 96:(part + 1) * 96]
-        return 0
-
-    lax.fori_loop(0, GROUP // TILE, project, 0)
-
-    lane = lax.broadcasted_iota(jnp.int32, (1, GROUP), 1)
-    image_index = jnp.zeros_like(lane)
-    for place, away in enumerate(IMAGE_ORDER):
-        base = d * GROUP + lax.rem(x + away, XS) * CHUNK - place * CHUNK
-        image_index = jnp.where(lane // CHUNK == place, base + lane, image_index)
-
     row_number = lax.broadcasted_iota(jnp.int32, (ROWS, 128), 0)
 
     def columns_of(step):
@@ -224,45 +299,100 @@
             mcol[0, rows, :] = column
             mcol[1, rows, :] = ((from_z * 2 + high) * 16 + m) * ROWS + row_number
 
+    w_behind.arrive()
+    w_on.start()
+    y_behind.start()
+    shares["s1"][0].start()
+    by_role(functools.partial(far, "f"), functools.partial(spread_other, "f"))
+    columns_of(0)
+    text_pass(2, 0)
+    y_own_in.arrive()
+    shares["s3"][0].start()
+    text_pass(1, 1)
+    w_far.arrive()
+    y_far.start()
+    shares["s2"][0].start()
+    by_role(functools.partial(finish, "f"), functools.partial(far, "f"))
+    columns_of(-1)
+    columns_of(1)
+    text_arrived(-3, 0)
+    text_forward(-3, 0, 1, 4)
+    y_behind_in.arrive()
+    shares["s4"][0].start()
+    text_pass(2, 1)
+    text_arrived(3, 0)
+    columns_of(-2)
+    columns_of(2)
+    pl.when(not_owner)(functools.partial(finish, "f"))
+    y_far_in.arrive()
+    shares["s5"][0].start()
+    complete("f")
+    for name in ("s1", "s2", "s3", "s4", "s5"):
+        shares[name][1].arrive(mine=False)
+    text_arrived(3, 1)
+    text_forward(3, 1, -1, 4)
+
+    def project(tile):
+        proj[pl.ds(tile * TILE, TILE), :] = lax.dot_general(
+            ff[tile], wf[...], (((0,), (0,)), ((), ())), preferred_element_type=f32
+        )
+
+    def normalize(tile):
+        for first in range(tile * TILE, (tile + 1) * TILE, 48):
+            rows = pl.ds(first, 48)
+            values = proj[rows, :]
+            unit[rows, :] = (values * inverse_norm(values)).astype(bf16)
+
     log2e = 1.4426950408889634
     scaling = scale_ref[0]
     slope, shift = scaling * log2e, bias_ref[0] * log2e
 
-    def coefficients_of(chunk):
-        for step in TEXT_ORDER[2 * chunk:2 * chunk + 2]:
-            columns_of(step)
-        rows = pl.ds(chunk * CHUNK, CHUNK)
-        logits[...] = lax.dot_general(
-            tn[rows, :], unit[...], (((1,), (1,)), ((), ())), preferred_element_type=f32
+    def products_of(buffer, chunk, tile):
+        logits[buffer] = lax.dot_general(
+            tn[pl.ds(chunk * CHUNK, CHUNK), :], unit[pl.ds(pl.multiple_of(tile * TILE, TILE), TILE), :],
+            (((1,), (1,)), ((), ())), preferred_element_type=f32,
         )
 
-        def coefficients(step, _):
-            at = pl.multiple_of(step * 16, 16)
-            here = pl.ds(chunk * CHUNK + at, 16)
-            match = mcol[0, here, 0:1]
-            index = mcol[1, here, 0:1]
+    def signs_of(buffer, chunk, tile):
+        images = pl.ds(pl.multiple_of(tile * TILE, TILE), TILE)
+        image_index = d * GROUP + tile * TILE + lax.broadcasted_iota(jnp.int32, (1, TILE), 1)
+        count = 16
+        for at in range(0, CHUNK, count):
+            here = pl.ds(chunk * CHUNK + at, count)
+            match = jnp.concatenate([mcol[0, here, :]] * (TILE // 128), axis=1)
+            index = jnp.concatenate([mcol[1, here, :]] * (TILE // 128), axis=1)
             positive = (index == image_index) | (match == image_index)
-            power = slope * logits[pl.ds(at, 16), :] + shift
+            power = slope * logits[buffer, pl.ds(at, count), :] + shift
             grown = 1.0 + jnp.exp2(jnp.where(positive, power, -power))
-            coef[here, :] = (
+            coef[here, images] = (
                 jnp.where(positive, -scaling, scaling) * pl.reciprocal(grown, approx=True)
             ).astype(bf16)
-            return 0
-
-        lax.fori_loop(0, CHUNK // 16, coefficients, 0)
-
-    coefficients_of(0)
-    coefficients_of(1)
+
+    def coefficients_of(*units):
+        for at, unit_at in enumerate(units):
+            if at == 0:
+                products_of(0, *unit_at)
+            if at + 1 < len(units):
+                products_of((at + 1) % 2, *units[at + 1])
+            signs_of(at % 2, *unit_at)
+
+    project(0)
+    project(1)
+    normalize(0)
+    project(2)
+    normalize(1)
+    normalize(2)
+    coefficients_of((0, 0), (0, 1), (0, 2), (1, 0), (1, 1), (1, 2))
     text_arrived(-3, 1)
-    coefficients_of(2)
+    columns_of(-3)
+    coefficients_of((2, 0), (2, 1), (2, 2))
     text_arrived(4, 0)
     text_arrived(4, 1)
-    coefficients_of(3)
-
-    parts = ((0, HEAD), (HEAD, BLOCK - HEAD))
+    columns_of(3)
+    columns_of(4)
 
     def image_tile(tile):
-        columns = pl.ds(tile * TILE, TILE)
+        columns = pl.ds(pl.multiple_of(tile * TILE, TILE), TILE)
         du[columns, :] = lax.dot_general(
             coef[:, columns], tn[...], (((0,), (0,)), ((), ())), preferred_element_type=f32
         )
@@ -271,8 +401,10 @@
         rows = pl.ds(chunk * CHUNK, CHUNK)
         dt[rows, :] = jnp.dot(coef[rows, :], unit[...], preferred_element_type=f32)
 
+    image_x = (far_x, right_x, left_x, x)
+
     def image_block(place, which, first=0, count=BLOCK):
-        return pl.ds(pl.multiple_of(place * CHUNK + which * BLOCK + first, 16), count)
+        return pl.ds(pl.multiple_of(image_x[place] * CHUNK + which * BLOCK + first, 16), count)
 
     def to_sibling(place):
         csend[place] = du[image_block(place, 1 - core), :].astype(bf16)
@@ -324,14 +456,21 @@
             ("ts", way, away, part), tout.at[place, pl.ds(first, count)], text_buffer(way, away, part), at_z(way)
         )
 
-    image_tile(0)
+    first_tile = jnp.where(far_x < 2, 0, 2)
+    products_of(0, 3, first_tile)
+    products_of(1, 3, 1)
+    signs_of(0, 3, first_tile)
+    products_of(0, 3, 2 - first_tile)
+    signs_of(1, 3, 1)
+    image_tile(first_tile)
+    signs_of(0, 3, 2 - first_tile)
+    image_tile(1)
     to_sibling(0)
-    image_tile(1)
-    to_sibling(1)
+    image_tile(2 - first_tile)
     arrived(("c", 0), crecv.at[0])
     image_send(0, 0, 1, xra)
     image_send(0, 1, -1, xlb)
-    image_tile(2)
+    to_sibling(1)
     to_sibling(2)
     to_sibling(3)
     arrived(("c", 1), crecv.at[1])
@@ -356,8 +495,6 @@
         first, count = (0, BLOCK) if part is None else parts[part]
         return gp.at[pl.ds(pl.multiple_of(from_x * CHUNK + which * BLOCK + first, 16), count)]
 
-    owner = ylo == core
-    not_owner = jnp.logical_not(owner)
     text_send(1, 2, 1)
     text_send(-1, 2, 0)
 
@@ -404,8 +541,6 @@
         start(("gr", part), block, block, at_x(1))
         start(("gl", part), block, block, at_x(-1))
         start(("gs", 0, part), block, block, sibling)
-
-    left_x, right_x, far_x = lax.rem(x + 3, XS), lax.rem(x + 1, XS), lax.rem(x + 2, XS)
 
     def gp_share(index, from_x, part):
         block = gp_block(from_x, core, part)
@@ -506,18 +641,22 @@
         columns = pl.ds((index % 3) * PIECE_COLS, PIECE_COLS)
         pg_ref[pl.ds(first, count), columns] = wa[index].astype(f32)[:count]
 
-    for copy in sent:
-        copy.wait_send()
+    for copy in sent.values():
+        (copy if isinstance(copy, Block) else copy()).wait_send()
 
     @pl.when(not_owner)
     def _():
         for part in range(2):
             to_owner(part).wait_send()
+        for name in gathered:
+            same("share", name, x, sibling).wait_send()
 
     @pl.when(owner)
     def _():
         for part in range(2):
             from_owner(part).wait_send()
+        for name in gathered:
+            same("across", name, x, other_ylo).wait_send()
 
     for index in range(PIECES):
         @pl.when(d != index)
@@ -539,9 +678,10 @@
     square = (GROUP, EMBED)
     tail = BLOCK - HEAD
     scratch = [
-        pltpu.VMEM((PAD, EMBED), bf16),
-        pltpu.VMEM((PAD, EMBED), bf16),
-        pltpu.VMEM((2,) + square, bf16),
+        pltpu.VMEM((2, PAD, EMBED), bf16),
+        pltpu.VMEM((2, PAD, EMBED), bf16),
+        pltpu.VMEM(square, bf16),
+        pltpu.VMEM((GROUP // TILE, GROUP, TILE), bf16),
         pltpu.VMEM((PAD, EMBED), bf16),
         pltpu.VMEM((PAD, EMBED), bf16),
         pltpu.VMEM((8, 128), jnp.int32),
@@ -551,7 +691,7 @@
         pltpu.VMEM((2, GROUP, 128), jnp.int32),
         pltpu.VMEM(square, f32),
         pltpu.VMEM(square, bf16),
-        pltpu.VMEM((CHUNK, GROUP), f32),
+        pltpu.VMEM((2, CHUNK, TILE), f32),
         pltpu.VMEM(square, bf16),
         pltpu.VMEM(square, f32),
         pltpu.VMEM(square, f32),

time: 119 us -> 111 us (0.933)
  Pallas kernels: 112 us -> 104 us
    pallas_call x1, Pallas kernels: 112 us -> 104 us  [local(): pl.pallas_call(kernel, out_shape=(jax.ShapeDtypeStruct((rows, EMBED), bf1...]
where the time goes in v3:
time: 111 us; the launch traced here: 109 us
  Pallas kernels  104 us (94%)
  local copies, waits for them, and re-layouts  3.05 us (3%)
  between operations  1.95 us (2%)
    pallas_call x1, Pallas kernels, local(): pl.pallas_call(kernel, out_shape=(jax.ShapeDtypeStruct((rows, EMBED), bf1...  104 us
    unnamed x7, local copies, waits for them, and re-layouts  3.05 us

profile of v3, /device:TPU:32, one launch (start us, length us, event | category | flops | bytes accessed | tf_op | source)
XLA Modules:
  0.0 109.3 jit_solution(16613458761491659008)
XLA Ops:
  1.9 104.3 %shard_map.85 = (bf16[72,1152]{1,0:T(8,128)(2,1)}, bf16[72,1152]{1,0:T(8,128)(2,1)}, f32[72,1152]{1,0:T(8,128)}) custom-call(f32[1]{0:T(128)S(6)} %copy.12.scale_ref, f32[1]{0:T(128)S(6)} %copy.13.bias_ref, bf16[72,1152]{1,0:T(8,128)(2,1)} %f_ref.1, bf16[72,1152]{1,0:T(8,128)(2,1)} %w_ref.1, bf16[72,1152]{1,0:T(8,128)(2,1)} %t_ref.1, s32[1,72]{1,0:T(1,128)} %bitcast.1), custom_call_target="tpu_custom_call" | custom-call | flops 12999999488 | bytes 1500000 | tf_op jit(solution)/shard_map/pallas_call | solution.py:723
  106.2 0.0 copy-start.1
  106.2 0.0 copy-start
  106.2 1.7 %copy.14 = bf16[72,1152]{1,0:T(8,128)(2,1)} copy(bf16[72,1152]{1,0:T(8,128)(2,1)} %get-tuple-element.6) | data formatting | bytes 331776
  107.9 0.0 copy-done.1
  107.9 0.7 copy.15
  108.5 0.0 copy-done
  108.5 0.7 copy.16
Async XLA Ops:
  106.2 1.7 %copy-start.1 = (bf16[72,1152]{1,0:T(8,128)(2,1)S(1)}, bf16[72,1152]{1,0:T(8,128)(2,1)}, u32[]{:S(2)}) copy-start(bf16[72,1152]{1,0:T(8,128)(2,1)} %get-tuple-element.7) | copy-start | bytes 497668
  106.2 2.3 %copy-start = (f32[72,1152]{1,0:T(8,128)S(1)}, f32[72,1152]{1,0:T(8,128)}, u32[]{:S(2)}) copy-start(f32[72,1152]{1,0:T(8,128)} %get-tuple-element.8) | copy-start | bytes 995332

commit v4 on v3

--- a/solution.py
+++ b/solution.py
@@ -16,7 +16,8 @@
 PAD = 80
 BLOCK = 144
 HEAD = 80
-NEAR = 64
+TEXT_PARTS = ((0, 64), (64, 48), (112, 32))
+FIRST = 48
 GROUP = 1152
 EMBED = 1152
 CHUNK = 288
@@ -24,7 +25,7 @@
 TEXT_ORDER = (0, -1, 1, -2, 2, -3, 3, 4)
 TEXT_POS = {step: at for at, step in enumerate(TEXT_ORDER)}
 PIECES, PIECE_ROWS, PIECE_COLS = 15, 16, 384
-SEMS = 224
+SEMS = 192
 
 
 def inverse_norm(values):
@@ -37,14 +38,25 @@
 
 
 def kernel(
-    scale_ref, bias_ref, f_ref, w_ref, t_ref, m_ref,
-    tg_ref, fg_ref, pg_ref,
+    scale_ref, bias_ref, f_in, w_in, t_in, m_in,
+    tg_out, fg_out, pg_out,
+    f_ref, w_ref, t_ref, m_ref, tg_ref, fg_ref, pg_ref,
     xsend, xrecv, wf, ff, tsend, trecv, msend, mrecv, tn, mt, mcol, proj, unit, logits, coef, dt, du,
     tout, tra, tlb, tr, tl, ysend_t, yrecv_t,
     csend, crecv, xout, xra, xlb, xr, xl, yout, yin, mine_sum, gp,
     ws, wr, wa,
-    send_sem, recv_sem,
+    send_sem, recv_sem, local_sem,
 ):
+    loads = [
+        pltpu.make_async_copy(source, held, local_sem.at[at])
+        for at, (source, held) in enumerate(((t_in, t_ref), (w_in, w_ref), (f_in, f_ref), (m_in, m_ref)))
+    ]
+    for load in loads:
+        load.start()
+
+    def store(at, held, target):
+        return pltpu.make_async_copy(held, target, local_sem.at[4 + at])
+
     d, m = lax.axis_index("dp"), lax.axis_index("mp")
     z, yhi = d // 2, d % 2
     x, ylo, core = m // 4, (m // 2) % 2, m % 2
@@ -93,6 +105,8 @@
     def arrived(name, dst, target=sibling):
         describe(name, dst, dst, target).wait_recv()
 
+    for load in loads:
+        load.wait()
     f_mine, w_mine = f_ref[...].astype(f32), w_ref[...].astype(f32)
     is_first = core == 0
     owner = ylo == core
@@ -113,23 +127,25 @@
     start("x0", xsend, xrecv, sibling)
 
     def text_rows(step, part):
-        first = TEXT_POS[step] * BLOCK
-        return pl.ds(first, NEAR) if part == 0 else pl.ds(first + NEAR, BLOCK - NEAR)
+        first, count = TEXT_PARTS[part]
+        return pl.ds(TEXT_POS[step] * BLOCK + first, count)
 
     def text_forward(step, part, way, new_step):
         start(("t", new_step, part), tn.at[text_rows(step, part)], tn.at[text_rows(new_step, part)], at_z(way))
-        if part == 1:
+        if part == 2:
             start(("m", new_step), mt.at[TEXT_POS[step]], mt.at[TEXT_POS[new_step]], at_z(way))
 
     def text_arrived(step, part):
         arrived(("t", step, part), tn.at[text_rows(step, part)])
-        if part == 1:
+        if part == 2:
             arrived(("m", step), mt.at[TEXT_POS[step]])
 
-    tn[pl.ds(0, NEAR), :] = text_mine[:NEAR].astype(bf16)
+    near = TEXT_PARTS[0][1]
+    tn[pl.ds(0, near), :] = text_mine[:near].astype(bf16)
     text_forward(0, 0, 1, -1)
     text_forward(0, 0, -1, 1)
-    start("t0", tsend, trecv, other_yhi)
+    start("t0", tsend.at[pl.ds(0, FIRST)], trecv.at[pl.ds(0, FIRST)], other_yhi)
+    start("t1", tsend.at[pl.ds(FIRST, PAD - FIRST)], trecv.at[pl.ds(FIRST, PAD - FIRST)], other_yhi)
     start("m0", msend, mrecv, other_yhi)
 
     def block_rows(from_x, which, part=None):
@@ -277,15 +293,21 @@
             text_forward(-way * step, part, way, -way * (step + 1))
 
     text_pass(1, 0)
-    arrived("t0", trecv)
+    arrived("t0", trecv.at[pl.ds(0, FIRST)])
+    taken = TEXT_PARTS[1][1] - (ROWS - near)
+    tn[text_rows(0, 1), :] = jnp.concatenate(
+        [tsend[...].astype(f32)[near:ROWS], trecv[pl.ds(0, FIRST), :].astype(f32)[:taken]]
+    ).astype(bf16)
+    text_forward(0, 1, 1, -1)
+    text_forward(0, 1, -1, 1)
+    arrived("t1", trecv.at[pl.ds(FIRST, PAD - FIRST)])
     arrived("m0", mrecv)
-    theirs = trecv[...].astype(f32)[:ROWS]
-    tn[text_rows(0, 1), :] = jnp.concatenate([tsend[...].astype(f32)[NEAR:ROWS], theirs]).astype(bf16)
+    tn[text_rows(0, 2), :] = trecv[...].astype(f32)[taken:ROWS].astype(bf16)
     mt[0, 0:1, :] = msend[0:1, :]
     mt[0, 1:2, :] = mrecv[0:1, :]
     mt[0, 2:8, :] = jnp.zeros((6, 128), jnp.int32)
-    text_forward(0, 1, 1, -1)
-    text_forward(0, 1, -1, 1)
+    text_forward(0, 2, 1, -1)
+    text_forward(0, 2, -1, 1)
 
     row_number = lax.broadcasted_iota(jnp.int32, (ROWS, 128), 0)
 
@@ -309,28 +331,30 @@
     y_own_in.arrive()
     shares["s3"][0].start()
     text_pass(1, 1)
+    text_pass(1, 2)
     w_far.arrive()
     y_far.start()
     shares["s2"][0].start()
+    text_arrived(-3, 0)
+    text_forward(-3, 0, 1, 4)
     by_role(functools.partial(finish, "f"), functools.partial(far, "f"))
     columns_of(-1)
     columns_of(1)
-    text_arrived(-3, 0)
-    text_forward(-3, 0, 1, 4)
+    text_pass(2, 1)
     y_behind_in.arrive()
     shares["s4"][0].start()
-    text_pass(2, 1)
+    text_pass(2, 2)
     text_arrived(3, 0)
     columns_of(-2)
     columns_of(2)
     pl.when(not_owner)(functools.partial(finish, "f"))
     y_far_in.arrive()
     shares["s5"][0].start()
+    text_arrived(3, 1)
+    text_forward(3, 1, -1, 4)
     complete("f")
     for name in ("s1", "s2", "s3", "s4", "s5"):
         shares[name][1].arrive(mine=False)
-    text_arrived(3, 1)
-    text_forward(3, 1, -1, 4)
 
     def project(tile):
         proj[pl.ds(tile * TILE, TILE), :] = lax.dot_general(
@@ -377,6 +401,8 @@
             signs_of(at % 2, *unit_at)
 
     project(0)
+    text_arrived(3, 2)
+    text_forward(3, 2, -1, 4)
     project(1)
     normalize(0)
     project(2)
@@ -384,10 +410,12 @@
     normalize(2)
     coefficients_of((0, 0), (0, 1), (0, 2), (1, 0), (1, 1), (1, 2))
     text_arrived(-3, 1)
+    text_arrived(-3, 2)
     columns_of(-3)
     coefficients_of((2, 0), (2, 1), (2, 2))
     text_arrived(4, 0)
     text_arrived(4, 1)
+    text_arrived(4, 2)
     columns_of(3)
     columns_of(4)
 
@@ -491,20 +519,12 @@
     text_send(-1, 3, 1)
     arrived(("c", 3), crecv.at[3])
 
-    def gp_block(from_x, which, part=None):
-        first, count = (0, BLOCK) if part is None else parts[part]
-        return gp.at[pl.ds(pl.multiple_of(from_x * CHUNK + which * BLOCK + first, 16), count)]
-
     text_send(1, 2, 1)
     text_send(-1, 2, 0)
 
     def to_owner(part):
         rows = pl.ds(*parts[part])
         return describe(("yo", part), yout.at[rows], yin.at[rows], other_ylo)
-
-    def from_owner(part):
-        block = gp_block(x, core, part)
-        return describe(("yg", part), block, block, other_ylo)
 
     for part in range(2):
         rows = pl.ds(*parts[part])
@@ -520,65 +540,71 @@
     text_send(1, 2, 0)
     text_send(-1, 2, 1)
 
-    for part in range(2):
-        @pl.when(owner)
-        def _(part=part):
+    def gp_copy(kind, tile, from_x, target, part=None):
+        block = gp.at[tile, block_rows(from_x, core, part)]
+        return describe((kind, tile, part), block, block, target)
+
+    def gp_move(kind, tile, from_x, target, part=None):
+        gp_copy(kind, tile, from_x, target, part).start()
+        sent[(kind, tile, part)] = functools.partial(gp_copy, kind, tile, from_x, target, part)
+
+    def gp_came(kind, tile, from_x, part=None):
+        gp_copy(kind, tile, from_x, sibling, part).wait_recv()
+
+    def gp_spread(tile):
+        gp_move("gr", tile, x, at_x(1))
+        gp_move("gl", tile, x, at_x(-1))
+        gp_move("gs", tile, x, sibling)
+
+    @pl.when(owner)
+    def _():
+        for part in range(2):
             first, count = parts[part]
             to_owner(part).wait_recv()
             total = mine_sum[pl.ds(first, count), :] + yin[pl.ds(first, count), :].astype(f32)
             projected = proj[image_block(3, core, first, count), :]
-            place = pl.multiple_of(x * CHUNK + core * BLOCK + first, 16)
-            gp[pl.ds(place, count), :] = norm_backward(
-                projected, inverse_norm(projected), total
-            ).astype(bf16)
-            from_owner(part).start()
-
-        @pl.when(not_owner)
-        def _(part=part):
-            from_owner(part).wait_recv()
-
-        block = gp_block(x, core, part)
-        start(("gr", part), block, block, at_x(1))
-        start(("gl", part), block, block, at_x(-1))
-        start(("gs", 0, part), block, block, sibling)
-
-    def gp_share(index, from_x, part):
-        block = gp_block(from_x, core, part)
-        start(("gs", index, part), block, block, sibling)
+            result = norm_backward(projected, inverse_norm(projected), total).astype(bf16)
+            for tile in range(tiles):
+                gp[tile, block_rows(x, core, part), :] = result[:, tile * TILE:(tile + 1) * TILE]
+        for tile in range(tiles):
+            gp_copy("yg", tile, x, other_ylo).start()
+            gp_spread(tile)
+
+    @pl.when(not_owner)
+    def _():
+        for tile in range(tiles):
+            gp_copy("yg", tile, x, other_ylo).wait_recv()
+            gp_spread(tile)
+
+    def gp_far(tile):
+        gp_came("gr", tile, left_x)
+        gp_move("gf", tile, left_x, at_x(1), 0)
+        gp_move("gs_left", tile, left_x, sibling)
+        gp_came("gl", tile, right_x)
+        gp_move("gf", tile, right_x, at_x(-1), 1)
+        gp_move("gs_right", tile, right_x, sibling)
+
+    def gp_finish(tile):
+        for part in range(2):
+            gp_came("gf", tile, far_x, part)
+            gp_move("gs_far", tile, far_x, sibling, part)
+
+    def gp_complete(tile):
+        for kind, from_x, part in (
+            ("gs", x, None), ("gs_left", left_x, None), ("gs_right", right_x, None),
+            ("gs_far", far_x, 0), ("gs_far", far_x, 1),
+        ):
+            block = gp.at[tile, block_rows(from_x, 1 - core, part)]
+            describe((kind, tile, part), block, block, sibling).wait_recv()
 
     text_send(1, 1, 1)
     text_send(-1, 1, 0)
-    block = gp_block(left_x, core, 0)
-    arrived(("gr", 0), block)
-    start("gfr", block, block, at_x(1))
-    gp_share(1, left_x, 0)
-    arrived(("gl", 0), gp_block(right_x, core, 0))
-    gp_share(2, right_x, 0)
-    block = gp_block(right_x, core, 1)
-    arrived(("gl", 1), block)
-    start("gfl", block, block, at_x(-1))
-    gp_share(2, right_x, 1)
-    arrived(("gr", 1), gp_block(left_x, core, 1))
-    gp_share(1, left_x, 1)
+    gp_far(0)
+    gp_far(1)
+    gp_finish(0)
+    gp_far(2)
     text_send(1, 1, 0)
     text_send(-1, 1, 1)
-    arrived("gfr", gp_block(far_x, core, 0))
-    gp_share(3, far_x, 0)
-    arrived("gfl", gp_block(far_x, core, 1))
-    gp_share(3, far_x, 1)
-
-    total = jnp.concatenate(
-        [text_partial(0, part) + text_came(1, 1, part) + text_came(-1, 1, part) for part in range(2)]
-    )
-    ysend_t[...] = jnp.concatenate([total[ROWS:], pad_rows]).astype(bf16)
-    start("ty", ysend_t, yrecv_t, other_yhi)
-
-    for part in range(2):
-        for index, from_x in enumerate((x, left_x, right_x, far_x)):
-            arrived(("gs", index, part), gp_block(from_x, 1 - core, part))
-
-    part = jnp.dot(f_ref[...], gp[...], preferred_element_type=f32)
-    ws[...] = jnp.concatenate([part, pad_rows]).astype(bf16)
 
     def piece_of(index):
         rows = pl.ds(pl.multiple_of((index // 3) * PIECE_ROWS, PIECE_ROWS), PIECE_ROWS)
@@ -591,8 +617,8 @@
             device_id=target, device_id_type=MESH,
         )
 
-    base = len(keys)
-    again = base + 16
+    base = SEMS - 32
+    again = SEMS - 16
 
     def scatter(index):
         rows, columns = piece_of(index)
@@ -601,21 +627,16 @@
     def gather(index):
         return numbered(again, index, d, wa.at[d], wa.at[d], dp_at(index))
 
-    for index in range(PIECES):
-        @pl.when(d != index)
-        def _(index=index):
-            scatter(index).start()
-
-    fg_ref[...] = lax.dot_general(
-        w_ref[...], gp[...], (((1,), (1,)), ((), ())), preferred_element_type=f32
-    ).astype(bf16)
-
-    arrived("ty", yrecv_t)
-    text_total = total[:ROWS] + yrecv_t[...].astype(f32)[:ROWS]
-    tg_ref[...] = norm_backward(text_values, text_inverse, text_total).astype(bf16)
-
-    @pl.when(d < PIECES)
-    def _():
+    def weight_tile(tile):
+        gp_complete(tile)
+        part = jnp.dot(f_ref[...], gp[tile], preferred_element_type=f32)
+        ws[:, tile * TILE:(tile + 1) * TILE] = jnp.concatenate([part, pad_rows[:, :TILE]]).astype(bf16)
+        for index in range(tile, PIECES, tiles):
+            @pl.when(d != index)
+            def _(index=index):
+                scatter(index).start()
+
+    def reduce_piece():
         rows, columns = piece_of(d)
         wr[d] = ws[rows, columns]
         for source in range(16):
@@ -631,6 +652,36 @@
             def _(index=index):
                 gather(index).start()
 
+    weight_tile(0)
+    gp_finish(1)
+    gp_finish(2)
+    weight_tile(1)
+
+    weight_tile(2)
+    pl.when((d < PIECES) & (d % 3 == 0))(reduce_piece)
+    feature = lax.dot_general(
+        w_ref[:, :TILE], gp[0], (((1,), (1,)), ((), ())), preferred_element_type=f32
+    )
+    for tile in range(1, tiles):
+        feature = feature + lax.dot_general(
+            w_ref[:, tile * TILE:(tile + 1) * TILE], gp[tile], (((1,), (1,)), ((), ())), preferred_element_type=f32
+        )
+    fg_ref[...] = feature.astype(bf16)
+    store(1, fg_ref, fg_out).start()
+
+    total = jnp.concatenate(
+        [text_partial(0, part) + text_came(1, 1, part) + text_came(-1, 1, part) for part in range(2)]
+    )
+    ysend_t[...] = jnp.concatenate([total[ROWS:], pad_rows]).astype(bf16)
+    start("ty", ysend_t, yrecv_t, other_yhi)
+
+    pl.when((d < PIECES) & (d % 3 != 0))(reduce_piece)
+
+    arrived("ty", yrecv_t)
+    text_total = total[:ROWS] + yrecv_t[...].astype(f32)[:ROWS]
+    tg_ref[...] = norm_backward(text_values, text_inverse, text_total).astype(bf16)
+    store(0, tg_ref, tg_out).start()
+
     for index in range(PIECES):
         @pl.when(d != index)
         def _(index=index):
@@ -641,6 +692,9 @@
         columns = pl.ds((index % 3) * PIECE_COLS, PIECE_COLS)
         pg_ref[pl.ds(first, count), columns] = wa[index].astype(f32)[:count]
 
+    store(2, pg_ref, pg_out).start()
+
+    assert len(keys) <= SEMS - 32
     for copy in sent.values():
         (copy if isinstance(copy, Block) else copy()).wait_send()
 
@@ -653,8 +707,8 @@
 
     @pl.when(owner)
     def _():
-        for part in range(2):
-            from_owner(part).wait_send()
+        for tile in range(tiles):
+            gp_copy("yg", tile, x, other_ylo).wait_send()
         for name in gathered:
             same("across", name, x, other_ylo).wait_send()
 
@@ -670,14 +724,24 @@
             def _(index=index):
                 gather(index).wait_send()
 
+    for at, (held, target) in enumerate(((tg_ref, tg_out), (fg_ref, fg_out), (pg_ref, pg_out))):
+        store(at, held, target).wait()
+
 
 def local(image_features, proj_weight, text_embed, text_match, logit_scale, logit_bias):
-    vmem = pl.BlockSpec(memory_space=pltpu.VMEM)
+    anywhere = pl.BlockSpec(memory_space=pl.ANY)
     smem = pl.BlockSpec(memory_space=pltpu.SMEM)
     block = (BLOCK, EMBED)
     square = (GROUP, EMBED)
     tail = BLOCK - HEAD
     scratch = [
+        pltpu.VMEM((ROWS, GROUP), bf16),
+        pltpu.VMEM((ROWS, EMBED), bf16),
+        pltpu.VMEM((ROWS, EMBED), bf16),
+        pltpu.VMEM((1, ROWS), jnp.int32),
+        pltpu.VMEM((ROWS, EMBED), bf16),
+        pltpu.VMEM((ROWS, GROUP), bf16),
+        pltpu.VMEM((ROWS, EMBED), f32),
         pltpu.VMEM((2, PAD, EMBED), bf16),
         pltpu.VMEM((2, PAD, EMBED), bf16),
         pltpu.VMEM(square, bf16),
@@ -712,12 +776,13 @@
         pltpu.VMEM(block, bf16),
         pltpu.VMEM(block, bf16),
         pltpu.VMEM(block, f32),
-        pltpu.VMEM(square, bf16),
+        pltpu.VMEM((GROUP // TILE, GROUP, TILE), bf16),
         pltpu.VMEM((PAD, EMBED), bf16),
         pltpu.VMEM((16, PIECE_ROWS, PIECE_COLS), bf16),
         pltpu.VMEM((16, PIECE_ROWS, PIECE_COLS), bf16),
         pltpu.SemaphoreType.DMA((SEMS,)),
         pltpu.SemaphoreType.DMA((SEMS,)),
+        pltpu.SemaphoreType.DMA((7,)),
     ]
     rows = text_embed.shape[0]
     return pl.pallas_call(
@@ -727,8 +792,8 @@
             jax.ShapeDtypeStruct((rows, GROUP), bf16),
             jax.ShapeDtypeStruct((rows, EMBED), f32),
         ),
-        in_specs=[smem, smem, vmem, vmem, vmem, vmem],
-        out_specs=(vmem, vmem, vmem),
+        in_specs=[smem, smem, anywhere, anywhere, anywhere, anywhere],
+        out_specs=(anywhere, anywhere, anywhere),
         scratch_shapes=scratch,
         compiler_params=pltpu.CompilerParams(
             collective_id=0, has_side_effects=True, vmem_limit_bytes=60 * 1024 * 1024

time: 111 us -> 109 us (0.982)
  no operation moved by 1% of the time
where the time goes in v4:
time: 109 us; the launch traced here: 108 us
  Pallas kernels  103 us (94%)
  local copies, waits for them, and re-layouts  3.05 us (3%)
  between operations  1.95 us (2%)
    pallas_call x1, Pallas kernels, local(): pl.pallas_call(kernel, out_shape=(jax.ShapeDtypeStruct((rows, EMBED), bf1...  103 us
    unnamed x7, local copies, waits for them, and re-layouts  3.05 us

profile of v4, /device:TPU:32, one launch (start us, length us, event | category | flops | bytes accessed | tf_op | source)
XLA Modules:
  0.0 108.4 jit_solution(15464699741291021692)
XLA Ops:
  1.9 103.4 %shard_map.85 = (bf16[72,1152]{1,0:T(8,128)(2,1)}, bf16[72,1152]{1,0:T(8,128)(2,1)}, f32[72,1152]{1,0:T(8,128)}) custom-call(f32[1]{0:T(128)S(6)} %copy.12.scale_ref, f32[1]{0:T(128)S(6)} %copy.13.bias_ref, bf16[72,1152]{1,0:T(8,128)(2,1)} %f_in.1, bf16[72,1152]{1,0:T(8,128)(2,1)} %w_in.1, bf16[72,1152]{1,0:T(8,128)(2,1)} %t_in.1, s32[1,72]{1,0:T(1,128)} %bitcast.1), custom_call_target="tpu_custom_call" | custom-call | flops 12999999488 | bytes 1500000 | tf_op jit(solution)/shard_map/pallas_call | solution.py:788
  105.3 0.0 copy-start.1
  105.3 0.0 copy-start
  105.3 1.7 %copy.14 = bf16[72,1152]{1,0:T(8,128)(2,1)} copy(bf16[72,1152]{1,0:T(8,128)(2,1)} %get-tuple-element.6) | data formatting | bytes 331776
  107.0 0.0 copy-done.1
  107.0 0.7 copy.15
  107.6 0.0 copy-done
  107.7 0.7 copy.16
Async XLA Ops:
  105.3 1.7 %copy-start.1 = (bf16[72,1152]{1,0:T(8,128)(2,1)S(1)}, bf16[72,1152]{1,0:T(8,128)(2,1)}, u32[]{:S(2)}) copy-start(bf16[72,1152]{1,0:T(8,128)(2,1)} %get-tuple-element.7) | copy-start | bytes 497668
  105.3 2.3 %copy-start = (f32[72,1152]{1,0:T(8,128)S(1)}, f32[72,1152]{1,0:T(8,128)}, u32[]{:S(2)}) copy-start(f32[72,1152]{1,0:T(8,128)} %get-tuple-element.8) | copy-start | bytes 995332

commit v5 on v4

--- a/solution.py
+++ b/solution.py
@@ -22,6 +22,7 @@
 EMBED = 1152
 CHUNK = 288
 TILE = 384
+PIECE = 96
 TEXT_ORDER = (0, -1, 1, -2, 2, -3, 3, 4)
 TEXT_POS = {step: at for at, step in enumerate(TEXT_ORDER)}
 PIECES, PIECE_ROWS, PIECE_COLS = 15, 16, 384
@@ -39,7 +40,7 @@
 
 def kernel(
     scale_ref, bias_ref, f_in, w_in, t_in, m_in,
-    tg_out, fg_out, pg_out,
+    all_out,
     f_ref, w_ref, t_ref, m_ref, tg_ref, fg_ref, pg_ref,
     xsend, xrecv, wf, ff, tsend, trecv, msend, mrecv, tn, mt, mcol, proj, unit, logits, coef, dt, du,
     tout, tra, tlb, tr, tl, ysend_t, yrecv_t,
@@ -47,6 +48,7 @@
     ws, wr, wa,
     send_sem, recv_sem, local_sem,
 ):
+    tg_out, fg_out, pg_out = (all_out.at[at] for at in range(3))
     loads = [
         pltpu.make_async_copy(source, held, local_sem.at[at])
         for at, (source, held) in enumerate(((t_in, t_ref), (w_in, w_ref), (f_in, f_ref), (m_in, m_ref)))
@@ -357,15 +359,22 @@
         shares[name][1].arrive(mine=False)
 
     def project(tile):
-        proj[pl.ds(tile * TILE, TILE), :] = lax.dot_general(
-            ff[tile], wf[...], (((0,), (0,)), ((), ())), preferred_element_type=f32
-        )
-
-    def normalize(tile):
-        for first in range(tile * TILE, (tile + 1) * TILE, 48):
-            rows = pl.ds(first, 48)
-            values = proj[rows, :]
-            unit[rows, :] = (values * inverse_norm(values)).astype(bf16)
+        values = lax.dot_general(ff[tile], wf[...], (((0,), (0,)), ((), ())), preferred_element_type=f32)
+        normal = (values * inverse_norm(values)).astype(bf16)
+        for part in range(TILE // PIECE):
+            piece = tile * (TILE // PIECE) + part
+            away = lax.rem(piece // (CHUNK // PIECE) - x + XS, XS)
+            place = jnp.where(away == 2, 0, jnp.where(away == 1, 1, jnp.where(away == 3, 2, 3)))
+            row = pl.multiple_of(place * CHUNK + (piece % (CHUNK // PIECE)) * PIECE, PIECE)
+            proj[pl.ds(row, PIECE), :] = values[part * PIECE:(part + 1) * PIECE]
+            unit[pl.ds(row, PIECE), :] = normal[part * PIECE:(part + 1) * PIECE]
+
+    image_x = (far_x, right_x, left_x, x)
+    lane = lax.broadcasted_iota(jnp.int32, (1, GROUP), 1)
+    image_number = jnp.zeros_like(lane)
+    for place, from_x in enumerate(image_x):
+        first = d * GROUP + (from_x - place) * CHUNK
+        image_number = jnp.where(lane // CHUNK == place, first + lane, image_number)
 
     log2e = 1.4426950408889634
     scaling = scale_ref[0]
@@ -379,7 +388,7 @@
 
     def signs_of(buffer, chunk, tile):
         images = pl.ds(pl.multiple_of(tile * TILE, TILE), TILE)
-        image_index = d * GROUP + tile * TILE + lax.broadcasted_iota(jnp.int32, (1, TILE), 1)
+        image_index = image_number[:, tile * TILE:(tile + 1) * TILE]
         count = 16
         for at in range(0, CHUNK, count):
             here = pl.ds(chunk * CHUNK + at, count)
@@ -404,10 +413,7 @@
     text_arrived(3, 2)
     text_forward(3, 2, -1, 4)
     project(1)
-    normalize(0)
     project(2)
-    normalize(1)
-    normalize(2)
     coefficients_of((0, 0), (0, 1), (0, 2), (1, 0), (1, 1), (1, 2))
     text_arrived(-3, 1)
     text_arrived(-3, 2)
@@ -429,10 +435,8 @@
         rows = pl.ds(chunk * CHUNK, CHUNK)
         dt[rows, :] = jnp.dot(coef[rows, :], unit[...], preferred_element_type=f32)
 
-    image_x = (far_x, right_x, left_x, x)
-
     def image_block(place, which, first=0, count=BLOCK):
-        return pl.ds(pl.multiple_of(image_x[place] * CHUNK + which * BLOCK + first, 16), count)
+        return pl.ds(pl.multiple_of(place * CHUNK + which * BLOCK + first, 16), count)
 
     def to_sibling(place):
         csend[place] = du[image_block(place, 1 - core), :].astype(bf16)
@@ -484,21 +488,20 @@
             ("ts", way, away, part), tout.at[place, pl.ds(first, count)], text_buffer(way, away, part), at_z(way)
         )
 
-    first_tile = jnp.where(far_x < 2, 0, 2)
-    products_of(0, 3, first_tile)
+    products_of(0, 3, 0)
     products_of(1, 3, 1)
-    signs_of(0, 3, first_tile)
-    products_of(0, 3, 2 - first_tile)
+    signs_of(0, 3, 0)
+    products_of(0, 3, 2)
+    image_tile(0)
+    to_sibling(0)
     signs_of(1, 3, 1)
-    image_tile(first_tile)
-    signs_of(0, 3, 2 - first_tile)
     image_tile(1)
-    to_sibling(0)
-    image_tile(2 - first_tile)
+    to_sibling(1)
     arrived(("c", 0), crecv.at[0])
     image_send(0, 0, 1, xra)
     image_send(0, 1, -1, xlb)
-    to_sibling(1)
+    signs_of(0, 3, 2)
+    image_tile(2)
     to_sibling(2)
     to_sibling(3)
     arrived(("c", 1), crecv.at[1])
@@ -690,7 +693,7 @@
         first = (index // 3) * PIECE_ROWS
         count = min(PIECE_ROWS, ROWS - first)
         columns = pl.ds((index % 3) * PIECE_COLS, PIECE_COLS)
-        pg_ref[pl.ds(first, count), columns] = wa[index].astype(f32)[:count]
+        pg_ref[pl.ds(first, count), columns] = wa[index][:count]
 
     store(2, pg_ref, pg_out).start()
 
@@ -741,7 +744,7 @@
         pltpu.VMEM((1, ROWS), jnp.int32),
         pltpu.VMEM((ROWS, EMBED), bf16),
         pltpu.VMEM((ROWS, GROUP), bf16),
-        pltpu.VMEM((ROWS, EMBED), f32),
+        pltpu.VMEM((ROWS, EMBED), bf16),
         pltpu.VMEM((2, PAD, EMBED), bf16),
         pltpu.VMEM((2, PAD, EMBED), bf16),
         pltpu.VMEM(square, bf16),
@@ -785,21 +788,18 @@
         pltpu.SemaphoreType.DMA((7,)),
     ]
     rows = text_embed.shape[0]
-    return pl.pallas_call(
+    grads = pl.pallas_call(
         kernel,
-        out_shape=(
-            jax.ShapeDtypeStruct((rows, EMBED), bf16),
-            jax.ShapeDtypeStruct((rows, GROUP), bf16),
-            jax.ShapeDtypeStruct((rows, EMBED), f32),
-        ),
+        out_shape=jax.ShapeDtypeStruct((3, rows, EMBED), bf16),
         in_specs=[smem, smem, anywhere, anywhere, anywhere, anywhere],
-        out_specs=(anywhere, anywhere, anywhere),
+        out_specs=anywhere,
         scratch_shapes=scratch,
         compiler_params=pltpu.CompilerParams(
             collective_id=0, has_side_effects=True, vmem_limit_bytes=60 * 1024 * 1024
         ),
         cost_estimate=pl.CostEstimate(flops=13_000_000_000, bytes_accessed=1_500_000, transcendentals=2_700_000),
     )(logit_scale, logit_bias, image_features, proj_weight, text_embed, text_match.reshape(1, rows))
+    return grads[0], grads[1], grads[2].astype(f32)
 
 
 def solution(mesh):

time: 109 us -> 107 us (0.982)
  local copies, waits for them, and re-layouts: 3.05 us -> 0 us
  other arithmetic: 0 us -> 1.93 us
    unnamed x7 -> x0, local copies, waits for them, and re-layouts: 3.05 us -> none
    convert_element_type x0 -> x1, other arithmetic: none -> 1.93 us  [local(): return (grads[0], grads[1], grads[2].astype(f32))]
where the time goes in v5:
time: 107 us
  Pallas kernels  103 us (96%)
  other arithmetic  1.93 us (2%)
  between operations  1.93 us (2%)
    pallas_call x1, Pallas kernels, local(): pl.pallas_call(kernel, out_shape=jax.ShapeDtypeStruct((3, rows, EMBED), b...  103 us

profile of v5, /device:TPU:32, one launch (start us, length us, event | category | flops | bytes accessed | tf_op | source)
XLA Modules:
  0.0 107.1 jit_solution(16361051494565139073)
XLA Ops:
  1.9 103.2 %shard_map.85 = bf16[3,72,1152]{2,1,0:T(8,128)(2,1)} custom-call(f32[1]{0:T(128)S(6)} %copy.9.scale_ref, f32[1]{0:T(128)S(6)} %copy.10.bias_ref, bf16[72,1152]{1,0:T(8,128)(2,1)} %f_in.1, bf16[72,1152]{1,0:T(8,128)(2,1)} %w_in.1, bf16[72,1152]{1,0:T(8,128)(2,1)} %t_in.1, s32[1,72]{1,0:T(1,128)} %bitcast.8), custom_call_target="tpu_custom_call" | custom-call | flops 12999999488 | bytes 1500000 | tf_op jit(solution)/shard_map/pallas_call | solution.py:791
  105.2 1.9 %bitcast_convert_fusion = (f32[72,1152]{1,0:T(8,128)}, bf16[72,1152]{1,0:T(8,128)(2,1)}, bf16[72,1152]{1,0:T(8,128)(2,1)}) fusion(bf16[3,72,1152]{2,1,0:T(8,128)(2,1)} %shard_map.85), kind=kLoop, calls=%fused_computation | loop fusion | flops 82944 | bytes 1161216 | tf_op jit(solution)/shard_map/convert_element_type | solution.py:802

commit v6 on v5

--- a/solution.py
+++ b/solution.py
@@ -650,10 +650,8 @@
         for source in range(1, 16):
             total = total + wr[source].astype(f32)
         wa[d] = total.astype(bf16)
-        for index in range(16):
-            @pl.when(d != index)
-            def _(index=index):
-                gather(index).start()
+        for step in (8, 7, 9, 6, 10, 5, 11, 4, 12, 3, 13, 2, 14, 1, 15):
+            gather(lax.rem(d + step, 16)).start()
 
     weight_tile(0)
     gp_finish(1)

time: 107 us -> 107 us (level)
  no operation moved by 1% of the time
where the time goes in v6:
time: 107 us
  Pallas kernels  103 us (96%)
  other arithmetic  1.93 us (2%)
  between operations  1.93 us (2%)
    pallas_call x1, Pallas kernels, local(): pl.pallas_call(kernel, out_shape=jax.ShapeDtypeStruct((3, rows, EMBED), b...  103 us

profile of v6, /device:TPU:32, one launch (start us, length us, event | category | flops | bytes accessed | tf_op | source)
XLA Modules:
  0.0 107.2 jit_solution(13232346611210590189)
XLA Ops:
  1.9 103.4 %shard_map.85 = bf16[3,72,1152]{2,1,0:T(8,128)(2,1)} custom-call(f32[1]{0:T(128)S(6)} %copy.9.scale_ref, f32[1]{0:T(128)S(6)} %copy.10.bias_ref, bf16[72,1152]{1,0:T(8,128)(2,1)} %f_in.1, bf16[72,1152]{1,0:T(8,128)(2,1)} %w_in.1, bf16[72,1152]{1,0:T(8,128)(2,1)} %t_in.1, s32[1,72]{1,0:T(1,128)} %bitcast.8), custom_call_target="tpu_custom_call" | custom-call | flops 12999999488 | bytes 1500000 | tf_op jit(solution)/shard_map/pallas_call | solution.py:789
  105.3 1.9 %bitcast_convert_fusion = (f32[72,1152]{1,0:T(8,128)}, bf16[72,1152]{1,0:T(8,128)(2,1)}, bf16[72,1152]{1,0:T(8,128)(2,1)}) fusion(bf16[3,72,1152]{2,1,0:T(8,128)(2,1)} %shard_map.85), kind=kLoop, calls=%fused_computation | loop fusion | flops 82944 | bytes 1161216 | tf_op jit(solution)/shard_map/convert_element_type | solution.py:800
